TPU v7x, 32 devices: a whole 2x2x4 slice. The times are simulated.
32 devices in a mesh: bore: 8 (over y, x, core), freq: 4 (over z).
Axes of the slice: x: 2, y: 2, z: 4, core: 2. Of those that a mesh axis runs over, the one named last changes fastest.
Arguments:
- loads: bfloat16 [128, 64, 8192], P('bore', None, 'freq'), may hold values from -48 to 48
- pair_spectra: bfloat16 [8, 2, 4096, 4096], P('freq', None, 'bore'), may hold values from -0.09375 to 0.09375
- share: bfloat16 [128, 4096], P(None, 'bore'), may hold values from 0.5 to 2
- assignment: int32 [4096], replicated, may hold values from 0 to 63, as said below
- freq_index: int32 [8], replicated, may hold values from 1 to 4095
Outputs:
- wall_temps: bfloat16 [128, 64, 8192], P(('bore', 'freq'))
Inputs may be any that keep to these rules, and one draw needn't show every extreme that they name: `assignment`: each of the 64 buildings is served by exactly 64 boreholes.
All inputs are finite; a program needn't handle non-finite values.
Results may differ from a plain program's by a relative error of at most 0.029.
Values may be sent and summed in bfloat16 or wider, within the bound.
A program may use at most 128 MiB of HBM per device.

v0:
```python
import functools
import math

import jax
import jax.numpy as jnp
from jax import lax
from jax.experimental import pallas as pl
from jax.experimental.pallas import tpu as pltpu
from jax.sharding import PartitionSpec as P

NBLD = 64
FLOC = 2
MESH = pl.DeviceIdType.MESH
NT = (((1,), (1,)), ((), ()))
TN = (((0,), (0,)), ((), ()))


def harmonic_column(freq_ref, freqs):
    row = lax.broadcasted_iota(jnp.int32, (freqs, 1), 0)
    column = jnp.zeros((freqs, 1), jnp.int32)
    for k in range(freqs):
        column = jnp.where(row == k, freq_ref[k], column)
    return column


def cos_sin(harmonics, first_hour, count, hours):
    freqs = harmonics.shape[0]
    t = lax.broadcasted_iota(jnp.int32, (freqs, count), 1) + first_hour
    phase = (harmonics * t) & (hours - 1)
    quarter = hours // 4
    turn = (phase + quarter // 2) // quarter
    x = (phase - turn * quarter).astype(jnp.float32) * (2.0 * math.pi / hours)
    y = x * x
    c = 1.0 + y * (-0.5 + y * (1 / 24 + y * (-1 / 720 + y * (1 / 40320 - y * (1 / 3628800)))))
    s = x * (1.0 + y * (-1 / 6 + y * (1 / 120 + y * (-1 / 5040 + y * (1 / 362880)))))
    odd = (turn & 1) == 1
    cos = jnp.where(odd, s, c)
    sin = jnp.where(odd, c, s)
    cos = jnp.where((turn == 1) | (turn == 2), -cos, cos)
    sin = jnp.where((turn == 2) | (turn == 3), -sin, sin)
    return cos, sin


def halves(x):
    upper = x.astype(jnp.bfloat16)
    return upper, (x - upper.astype(jnp.float32)).astype(jnp.bfloat16)


def superpose_kernel(
    nb, nz, hours, freq_ref, owner_ref, loads_hbm, pair_hbm, share_hbm, out_ref,
    loads_v, pair_v, share_v, sel_v, grid_v, spec_v,
    rs_stage, rs_recv, bs_all, wall_stage, wall_recv, a_stage, a_recv,
    loads_sem, pair_sem, own_sem, sh_send, sh_recv, fw_send, fw_recv,
    rs_ssem, rs_rsem, bs_ssem, bs_rsem, wl_ssem, wl_rsem, a_ssem, a_rsem,
):
    b = lax.axis_index("bore")
    z = lax.axis_index("freq")
    sloc = loads_hbm.shape[0]
    tloc = loads_hbm.shape[2]
    freqs = freq_ref.shape[0]
    bores = owner_ref.shape[1]
    bloc = pair_hbm.shape[2]
    s4 = sloc // nz
    core = b % 2
    chip = b // 2
    chips = nb // 2
    sibling = b + 1 - 2 * core

    barrier = pltpu.get_barrier_semaphore()
    for r in range(1, nb):
        pl.semaphore_signal(barrier, inc=1, device_id=((b + r) % nb, z), device_id_type=MESH)
    for r in range(1, nz):
        pl.semaphore_signal(barrier, inc=1, device_id=(b, (z + r) % nz), device_id_type=MESH)

    parts = loads_sem.shape[0]
    sp = sloc // parts
    load_copies = [
        pltpu.make_async_copy(loads_hbm.at[pl.ds(i * sp, sp)], loads_v.at[pl.ds(i * sp, sp)], loads_sem.at[i])
        for i in range(parts)
    ]
    for copy in load_copies:
        copy.start()
    own_share = pltpu.make_async_copy(share_hbm, share_v.at[b], own_sem)
    own_share.start()
    pair_copies = [
        pltpu.make_async_copy(pair_hbm.at[f, d], pair_v.at[f, d], pair_sem.at[f, d])
        for f in range(FLOC)
        for d in range(2)
    ]

    cos, sin = cos_sin(harmonic_column(freq_ref, freqs), z * tloc, tloc, hours)
    table = jnp.concatenate([*halves(cos), *halves(sin)], 0)
    to = lax.broadcasted_iota(jnp.int32, (2 * freqs, 4 * freqs), 0)
    part = lax.broadcasted_iota(jnp.int32, (2 * freqs, 4 * freqs), 1)
    same = (to % freqs == part % freqs) & (to // freqs == part // (2 * freqs))
    join = jnp.where(same, jnp.where(to < freqs, 1.0, -1.0), 0.0).astype(jnp.bfloat16)

    pl.semaphore_wait(barrier, nb - 1 + nz - 1)

    share_copies = []
    for r in range(1, chips):
        share_copies.append(
            pltpu.make_async_remote_copy(
                src_ref=share_hbm, dst_ref=share_v.at[b], send_sem=sh_send.at[r], recv_sem=sh_recv.at[r],
                device_id=((chip + r) % chips * 2 + core, z), device_id_type=MESH,
            )
        )
    share_copies.append(
        pltpu.make_async_remote_copy(
            src_ref=share_hbm, dst_ref=share_v.at[b], send_sem=sh_send.at[0], recv_sem=sh_recv.at[0],
            device_id=(sibling, z), device_id_type=MESH,
        )
    )
    for copy in share_copies:
        copy.start()

    for i, copy in enumerate(load_copies):
        copy.wait()
        if i < len(pair_copies):
            pair_copies[i].start()
        chunk = loads_v[pl.ds(i * sp, sp)].reshape(sp * NBLD, tloc)
        x = lax.dot_general(chunk, table, NT, preferred_element_type=jnp.float32)
        upper, lower = halves(x)
        spec_v[:, pl.ds(i * sp * NBLD, sp * NBLD)] = (
            lax.dot_general(join, upper, NT, preferred_element_type=jnp.float32)
            + lax.dot_general(join, lower, NT, preferred_element_type=jnp.float32)
        ) * (1.0 / math.sqrt(hours))
    for copy in pair_copies[parts:]:
        copy.start()

    lanes = sloc * NBLD
    keep = lax.broadcasted_iota(jnp.int32, (sloc, lanes), 1) // NBLD == lax.broadcasted_iota(
        jnp.int32, (sloc, lanes), 0
    )
    fold_from = lax.broadcasted_iota(jnp.int32, (lanes, 128), 0) % NBLD
    fold_to = lax.broadcasted_iota(jnp.int32, (lanes, 128), 1)
    folded = jnp.zeros((nz * 2 * sloc, 128), jnp.float32)
    for f in range(FLOC):
        spread = jnp.concatenate(
            [
                jnp.where(keep, spec_v[pl.ds(c * freqs + k * FLOC + f, 1), :], 0.0).astype(jnp.bfloat16)
                for k in range(nz)
                for c in range(2)
            ],
            0,
        )
        fold = (fold_from + f * NBLD == fold_to).astype(jnp.float32).astype(jnp.bfloat16)
        folded = folded + jnp.dot(spread, fold, preferred_element_type=jnp.float32)
    rs_stage[...] = folded.astype(jnp.bfloat16).reshape(nz, 2 * sloc, 128)

    rs_copies = []
    for r in range(1, nz):
        to = (z + r) % nz
        rs_copies.append(
            pltpu.make_async_remote_copy(
                src_ref=rs_stage.at[to], dst_ref=rs_recv.at[z], send_sem=rs_ssem.at[r], recv_sem=rs_rsem.at[r],
                device_id=(b, to), device_id_type=MESH,
            )
        )
        rs_copies[-1].start()
    rs_recv[z] = rs_stage[z]

    for q in range(nb):
        piece = pl.ds(q * bloc, bloc)
        label = lax.broadcasted_iota(jnp.int32, (2 * NBLD, bloc), 0) % NBLD
        sel_v[:, piece] = (label == owner_ref[:, piece]).astype(jnp.float32).astype(jnp.bfloat16)

    here = sel_v[0:NBLD, pl.ds(pl.multiple_of(b * bloc, 128), bloc)]
    width = 1024

    def gather_rows(f):
        for d in range(2):
            pair_copies[2 * f + d].wait()

            def step(i, carry):
                piece = pl.ds(pl.multiple_of(i * width, width), width)
                total = jnp.dot(here, pair_v[f, d, :, piece], preferred_element_type=jnp.float32)
                grid_v[f, pl.ds(d * NBLD, NBLD), piece] = total.astype(jnp.bfloat16)
                return carry

            lax.fori_loop(0, bores // width, step, 0)

    gather_rows(0)

    for copy in rs_copies:
        copy.wait_recv()
    spec = rs_recv[0].astype(jnp.float32)
    for k in range(1, nz):
        spec = spec + rs_recv[k].astype(jnp.float32)
    bs_all[b] = spec.astype(jnp.bfloat16)
    bs_copies = []
    for r in range(1, nb):
        bs_copies.append(
            pltpu.make_async_remote_copy(
                src_ref=bs_all.at[b], dst_ref=bs_all.at[b], send_sem=bs_ssem.at[r], recv_sem=bs_rsem.at[r],
                device_id=((b + r) % nb, z), device_id_type=MESH,
            )
        )
        bs_copies[-1].start()

    fw_copies = []
    for r in range(1, chips):
        share_copies[r - 1].wait_recv()
        origin = (chip + chips - r) % chips * 2 + core
        fw_copies.append(
            pltpu.make_async_remote_copy(
                src_ref=share_v.at[origin], dst_ref=share_v.at[origin], send_sem=fw_send.at[r], recv_sem=fw_recv.at[r],
                device_id=(sibling, z), device_id_type=MESH,
            )
        )
        fw_copies[-1].start()

    gather_rows(1)

    own_share.wait()
    share_copies[-1].wait_recv()
    for copy in bs_copies:
        copy.wait_recv()
    for copy in fw_copies:
        copy.wait_recv()

    rows = nb * 2 * sloc
    spec_all = bs_all[...].reshape(rows, 128).astype(jnp.float32)
    half = lax.broadcasted_iota(jnp.int32, (rows, 128), 1) // NBLD
    spec_f = [jnp.where(half == f, spec_all, 0.0).astype(jnp.bfloat16) for f in range(FLOC)]

    def source_step(q, walls):
        piece = pl.ds(pl.multiple_of(q * bloc, 128), bloc)
        select = sel_v[:, piece]
        weight = share_v[q].astype(jnp.float32).reshape(nb, 1, sloc, bloc)
        new = []
        for f in range(FLOC):
            picked = jnp.dot(spec_f[f], select, preferred_element_type=jnp.float32)
            source = (picked.reshape(nb, 2, sloc, bloc) * weight).astype(jnp.bfloat16).reshape(rows, bloc)
            new.append(
                walls[f] + lax.dot_general(source, grid_v[f, :, piece], NT, preferred_element_type=jnp.float32)
            )
        return tuple(new)

    walls = lax.fori_loop(0, nb, source_step, tuple(jnp.zeros((rows, 128), jnp.float32) for _ in range(FLOC)), unroll=8)
    sign = jnp.where(lax.broadcasted_iota(jnp.int32, (nb * sloc, 128), 1) < NBLD, -1.0, 1.0)
    for f in range(FLOC):
        crossed = walls[f].reshape(nb, 2, sloc, 128)
        real = crossed[:, 0].reshape(nb * sloc, 128)
        imag = crossed[:, 1].reshape(nb * sloc, 128)
        joined = real + sign * pltpu.roll(imag, NBLD, 1)
        wall_stage[:, f] = joined.astype(jnp.bfloat16).reshape(nb, sloc, 128)

    wl_copies = []
    for r in range(1, nb):
        to = (b + r) % nb
        wl_copies.append(
            pltpu.make_async_remote_copy(
                src_ref=wall_stage.at[to], dst_ref=wall_recv.at[b], send_sem=wl_ssem.at[r], recv_sem=wl_rsem.at[r],
                device_id=(to, z), device_id_type=MESH,
            )
        )
        wl_copies[-1].start()
    wall_recv[b] = wall_stage[b]
    for copy in wl_copies:
        copy.wait_recv()
    wall = wall_recv[0].astype(jnp.float32)
    for q in range(1, nb):
        wall = wall + wall_recv[q].astype(jnp.float32)
    wall = wall * (NBLD / bores)
    for k in range(nz):
        for f in range(FLOC):
            a_stage[k, f * s4 : (f + 1) * s4, :] = wall[f, k * s4 : (k + 1) * s4, :]

    a_copies = []
    for r in range(1, nz):
        to = (z + r) % nz
        a_copies.append(
            pltpu.make_async_remote_copy(
                src_ref=a_stage.at[to], dst_ref=a_recv.at[z], send_sem=a_ssem.at[r], recv_sem=a_rsem.at[r],
                device_id=(b, to), device_id_type=MESH,
            )
        )
        a_copies[-1].start()
    a_recv[z] = a_stage[z]
    for copy in share_copies + rs_copies + bs_copies + fw_copies + wl_copies:
        copy.wait_send()
    for copy in a_copies:
        copy.wait()
    out_ref[...] = a_recv[...].reshape(nz * FLOC * s4, 128)


def superpose(loads, pair_spectra, share, owners, freq_index, nb, nz):
    sloc, _, tloc = loads.shape
    bloc, bores = pair_spectra.shape[2:]
    scenarios = share.shape[0]
    freqs = freq_index.shape[0]
    s4 = sloc // nz
    bf16, f32, dma = jnp.bfloat16, jnp.float32, pltpu.SemaphoreType.DMA
    anywhere = pl.BlockSpec(memory_space=pl.ANY)
    return pl.pallas_call(
        functools.partial(superpose_kernel, nb, nz, tloc * nz),
        out_shape=jax.ShapeDtypeStruct((nz * FLOC * s4, 128), f32),
        in_specs=[
            pl.BlockSpec(memory_space=pltpu.SMEM),
            pl.BlockSpec(memory_space=pltpu.VMEM),
            anywhere,
            anywhere,
            anywhere,
        ],
        out_specs=pl.BlockSpec(memory_space=pltpu.VMEM),
        scratch_shapes=[
            pltpu.VMEM(loads.shape, bf16),
            pltpu.VMEM(pair_spectra.shape, bf16),
            pltpu.VMEM((nb, scenarios, bloc), bf16),
            pltpu.VMEM((2 * NBLD, bores), bf16),
            pltpu.VMEM((FLOC, 2 * NBLD, bores), bf16),
            pltpu.VMEM((2 * freqs, sloc * NBLD), f32),
            pltpu.VMEM((nz, 2 * sloc, 128), bf16),
            pltpu.VMEM((nz, 2 * sloc, 128), bf16),
            pltpu.VMEM((nb, 2 * sloc, 128), bf16),
            pltpu.VMEM((nb, FLOC, sloc, 128), bf16),
            pltpu.VMEM((nb, FLOC, sloc, 128), bf16),
            pltpu.VMEM((nz, FLOC * s4, 128), f32),
            pltpu.VMEM((nz, FLOC * s4, 128), f32),
            dma((4,)),
            dma((FLOC, 2)),
            dma,
            dma((nb // 2,)),
            dma((nb // 2,)),
            dma((nb // 2,)),
            dma((nb // 2,)),
            dma((nz,)),
            dma((nz,)),
            dma((nb,)),
            dma((nb,)),
            dma((nb,)),
            dma((nb,)),
            dma((nz,)),
            dma((nz,)),
        ],
        compiler_params=pltpu.CompilerParams(
            collective_id=0, has_side_effects=True, vmem_limit_bytes=56 * 2**20
        ),
        name="superpose",
    )(freq_index, owners, loads, pair_spectra, share)


def inverse_kernel(hours, freq_ref, wall_hbm, out_hbm, wall_v, right_v, out_v, in_sem, out_sem):
    freqs = freq_ref.shape[0]
    s4 = out_hbm.shape[0]
    parts = out_sem.shape[0]
    count = hours // parts
    fetch = pltpu.make_async_copy(wall_hbm, wall_v, in_sem)
    fetch.start()
    harmonics = harmonic_column(freq_ref, freqs)

    def fill(i, carry):
        piece = pl.ds(pl.multiple_of(i * count, count), count)
        cos, sin = cos_sin(harmonics, i * count, count, hours)
        upper, lower = halves(jnp.concatenate([cos, sin], 0))
        right_v[:, piece] = jnp.concatenate([upper, lower, upper], 0)
        return carry

    lax.fori_loop(0, parts, fill, 0)
    fetch.wait()
    low = lax.broadcasted_iota(jnp.int32, (freqs, 128), 1) < NBLD
    real, imag = [], []
    for s in range(0, s4, 2):
        one = wall_v[pl.ds(s, freqs, stride=s4), :]
        two = wall_v[pl.ds(s + 1, freqs, stride=s4), :]
        real.append(jnp.where(low, one, pltpu.roll(two, NBLD, 1)))
        imag.append(jnp.where(low, pltpu.roll(one, NBLD, 1), two))
    left = jnp.concatenate([jnp.concatenate(real, 1), -jnp.concatenate(imag, 1)], 0)
    upper, lower = halves(left * (1.0 / math.sqrt(freqs)))
    upper, lower = upper.astype(jnp.float32), lower.astype(jnp.float32)
    left = jnp.concatenate([upper, upper, lower], 0).T.astype(jnp.bfloat16)
    width = min(512, count)
    copies = []
    for i in range(parts):
        for j in range(i * count, (i + 1) * count, width):
            total = jnp.dot(left, right_v[:, pl.ds(j, width)], preferred_element_type=jnp.float32)
            out_v[:, :, pl.ds(j, width)] = total.astype(jnp.bfloat16).reshape(s4, NBLD, width)
        piece = pl.ds(i * count, count)
        copies.append(pltpu.make_async_copy(out_v.at[:, :, piece], out_hbm.at[:, :, piece], out_sem.at[i]))
        copies[-1].start()
    for copy in copies:
        copy.wait()


def inverse(freq_index, wall, s4, hours):
    freqs = freq_index.shape[0]
    parts = 8
    return pl.pallas_call(
        functools.partial(inverse_kernel, hours),
        out_shape=jax.ShapeDtypeStruct((s4, NBLD, hours), jnp.bfloat16),
        in_specs=[pl.BlockSpec(memory_space=pltpu.SMEM), pl.BlockSpec(memory_space=pl.ANY)],
        out_specs=pl.BlockSpec(memory_space=pl.ANY),
        scratch_shapes=[
            pltpu.VMEM(wall.shape, jnp.float32),
            pltpu.VMEM((6 * freqs, hours), jnp.bfloat16),
            pltpu.VMEM((s4, NBLD, hours), jnp.bfloat16),
            pltpu.SemaphoreType.DMA,
            pltpu.SemaphoreType.DMA((parts,)),
        ],
        compiler_params=pltpu.CompilerParams(vmem_limit_bytes=56 * 2**20),
        name="inverse",
    )(freq_index, wall)


def solution(mesh):
    nb, nz = mesh.shape["bore"], mesh.shape["freq"]

    def body(loads, pair_spectra, share, assignment, freq_index):
        owners = assignment.reshape(1, -1)
        wall = superpose(loads, pair_spectra, share, owners, freq_index, nb, nz)
        return inverse(freq_index, wall, loads.shape[0] // nz, loads.shape[2] * nz)

    return jax.shard_map(
        body,
        mesh=mesh,
        in_specs=(
            P("bore", None, "freq"),
            P("freq", None, "bore", None),
            P(None, "bore"),
            P(),
            P(),
        ),
        out_specs=P(("bore", "freq"), None, None),
        check_vma=False,
    )
```

profile of v0, /device:TPU:0, one launch (start us, length us, event | category | flops | bytes accessed | tf_op | source)
XLA Modules:
  0.0 31.3 jit_solution(5211356450294831145)
XLA Ops:
  0.0 27.4 %superpose.1.wall_hbm = f32[32,128]{1,0:T(8,128)} custom-call(s32[8]{0:T(128)} %freq_ref.3, s32[1,4096]{1,0:T(1,128)} %bitcast.1, bf16[16,64,2048]{2,1,0:T(8,128)(2,1)} %loads_hbm.1, bf16[2,2,512,4096]{3,2,1,0:T(8,128)(2,1)} %pair_hbm.1, bf16[128,512]{1,0:T(8,128)(2,1)} %share_hbm.1), custom_call_target="tpu_custom_call" | custom-call | tf_op jit(solution)/shard_map/superpose/pallas_call | solution.py:296
  27.4 3.9 %inverse.1 = bf16[4,64,8192]{2,1,0:T(8,128)(2,1)} custom-call(s32[8]{0:T(128)} %freq_ref.3, f32[32,128]{1,0:T(8,128)} %superpose.1.wall_hbm), custom_call_target="tpu_custom_call" | custom-call | tf_op jit(solution)/shard_map/inverse/pallas_call | solution.py:389
where the time goes:
time: 31.6 us; the launch traced here: 31.3 us
  Pallas kernels  31.3 us (99%)
    pallas_call x1, Pallas kernels, superpose(): pl.pallas_call(functools.partial(superpose_kernel, nb, nz, tloc * nz), ou...  27.4 us
    pallas_call x1, Pallas kernels, inverse(): pl.pallas_call(functools.partial(inverse_kernel, hours), out_shape=jax.Sh...  3.86 us

commit v1 on v0

--- a/solution.py
+++ b/solution.py
@@ -23,9 +23,9 @@
     return column
 
 
-def cos_sin(harmonics, first_hour, count, hours):
+def cos_sin(harmonics, first_hour, count, hours, stride=1):
     freqs = harmonics.shape[0]
-    t = lax.broadcasted_iota(jnp.int32, (freqs, count), 1) + first_hour
+    t = lax.broadcasted_iota(jnp.int32, (freqs, count), 1) * stride + first_hour
     phase = (harmonics * t) & (hours - 1)
     quarter = hours // 4
     turn = (phase + quarter // 2) // quarter
@@ -295,7 +295,7 @@
     anywhere = pl.BlockSpec(memory_space=pl.ANY)
     return pl.pallas_call(
         functools.partial(superpose_kernel, nb, nz, tloc * nz),
-        out_shape=jax.ShapeDtypeStruct((nz * FLOC * s4, 128), f32),
+        out_shape=pltpu.VMEM((nz * FLOC * s4, 128), f32),
         in_specs=[
             pl.BlockSpec(memory_space=pltpu.SMEM),
             pl.BlockSpec(memory_space=pltpu.VMEM),
@@ -341,24 +341,14 @@
     )(freq_index, owners, loads, pair_spectra, share)
 
 
-def inverse_kernel(hours, freq_ref, wall_hbm, out_hbm, wall_v, right_v, out_v, in_sem, out_sem):
+def inverse_kernel(hours, freq_ref, wall_v, out_hbm, out_v, out_sem):
     freqs = freq_ref.shape[0]
     s4 = out_hbm.shape[0]
     parts = out_sem.shape[0]
     count = hours // parts
-    fetch = pltpu.make_async_copy(wall_hbm, wall_v, in_sem)
-    fetch.start()
     harmonics = harmonic_column(freq_ref, freqs)
-
-    def fill(i, carry):
-        piece = pl.ds(pl.multiple_of(i * count, count), count)
-        cos, sin = cos_sin(harmonics, i * count, count, hours)
-        upper, lower = halves(jnp.concatenate([cos, sin], 0))
-        right_v[:, piece] = jnp.concatenate([upper, lower, upper], 0)
-        return carry
-
-    lax.fori_loop(0, parts, fill, 0)
-    fetch.wait()
+    base_cos, base_sin = cos_sin(harmonics, 0, count, hours)
+    turn_cos, turn_sin = cos_sin(harmonics, 0, 128, hours, count)
     low = lax.broadcasted_iota(jnp.int32, (freqs, 128), 1) < NBLD
     real, imag = [], []
     for s in range(0, s4, 2):
@@ -373,9 +363,15 @@
     width = min(512, count)
     copies = []
     for i in range(parts):
-        for j in range(i * count, (i + 1) * count, width):
-            total = jnp.dot(left, right_v[:, pl.ds(j, width)], preferred_element_type=jnp.float32)
-            out_v[:, :, pl.ds(j, width)] = total.astype(jnp.bfloat16).reshape(s4, NBLD, width)
+        c, s = turn_cos[:, i : i + 1], turn_sin[:, i : i + 1]
+        for j in range(0, count, width):
+            piece = slice(j, j + width)
+            cos = base_cos[:, piece] * c - base_sin[:, piece] * s
+            sin = base_sin[:, piece] * c + base_cos[:, piece] * s
+            upper, lower = halves(jnp.concatenate([cos, sin], 0))
+            right = jnp.concatenate([upper, lower, upper], 0)
+            total = jnp.dot(left, right, preferred_element_type=jnp.float32)
+            out_v[:, :, pl.ds(i * count + j, width)] = total.astype(jnp.bfloat16).reshape(s4, NBLD, width)
         piece = pl.ds(i * count, count)
         copies.append(pltpu.make_async_copy(out_v.at[:, :, piece], out_hbm.at[:, :, piece], out_sem.at[i]))
         copies[-1].start()
@@ -384,23 +380,19 @@
 
 
 def inverse(freq_index, wall, s4, hours):
-    freqs = freq_index.shape[0]
     parts = 8
     return pl.pallas_call(
         functools.partial(inverse_kernel, hours),
         out_shape=jax.ShapeDtypeStruct((s4, NBLD, hours), jnp.bfloat16),
-        in_specs=[pl.BlockSpec(memory_space=pltpu.SMEM), pl.BlockSpec(memory_space=pl.ANY)],
+        in_specs=[pl.BlockSpec(memory_space=pltpu.SMEM), pl.BlockSpec(memory_space=pltpu.VMEM)],
         out_specs=pl.BlockSpec(memory_space=pl.ANY),
         scratch_shapes=[
-            pltpu.VMEM(wall.shape, jnp.float32),
-            pltpu.VMEM((6 * freqs, hours), jnp.bfloat16),
             pltpu.VMEM((s4, NBLD, hours), jnp.bfloat16),
-            pltpu.SemaphoreType.DMA,
             pltpu.SemaphoreType.DMA((parts,)),
         ],
         compiler_params=pltpu.CompilerParams(vmem_limit_bytes=56 * 2**20),
         name="inverse",
-    )(freq_index, wall)
+    )(freq_index, pltpu.with_memory_space_constraint(wall, pltpu.VMEM))
 
 
 def solution(mesh):

time: 31.6 us -> 30.3 us (0.959)
  Pallas kernels: 31.3 us -> 30 us
    pallas_call x1, Pallas kernels: 3.86 us -> 3.18 us  [inverse(): pl.pallas_call(functools.partial(inverse_kernel, hours), out_shape=jax.Sh...]
    pallas_call x1, Pallas kernels: 27.4 us -> 26.8 us  [superpose(): pl.pallas_call(functools.partial(superpose_kernel, nb, nz, tloc * nz), ou...]
where the time goes in v1:
time: 30.3 us; the launch traced here: 30 us
  Pallas kernels  30 us (99%)
    pallas_call x1, Pallas kernels, superpose(): pl.pallas_call(functools.partial(superpose_kernel, nb, nz, tloc * nz), ou...  26.8 us
    pallas_call x1, Pallas kernels, inverse(): pl.pallas_call(functools.partial(inverse_kernel, hours), out_shape=jax.Sh...  3.18 us

profile of v1, /device:TPU:0, one launch (start us, length us, event | category | flops | bytes accessed | tf_op | source)
XLA Modules:
  0.0 30.0 jit_solution(2452044720003930740)
XLA Ops:
  0.0 26.8 %superpose.1.wall_v = f32[32,128]{1,0:T(8,128)S(1)} custom-call(s32[8]{0:T(128)} %freq_ref.3, s32[1,4096]{1,0:T(1,128)} %bitcast.1, bf16[16,64,2048]{2,1,0:T(8,128)(2,1)} %loads_hbm.1, bf16[2,2,512,4096]{3,2,1,0:T(8,128)(2,1)} %pair_hbm.1, bf16[128,512]{1,0:T(8,128)(2,1)} %share_hbm.1), custom_call_target="tpu_custom_call" | custom-call | tf_op jit(solution)/shard_map/superpose/pallas_call | solution.py:296
  26.8 3.2 %inverse.1 = bf16[4,64,8192]{2,1,0:T(8,128)(2,1)} custom-call(s32[8]{0:T(128)} %freq_ref.3, f32[32,128]{1,0:T(8,128)S(1)} %superpose.1.wall_v), custom_call_target="tpu_custom_call" | custom-call | tf_op jit(solution)/shard_map/inverse/pallas_call | solution.py:384

commit v2 on v1

--- a/solution.py
+++ b/solution.py
@@ -48,10 +48,10 @@
 
 def superpose_kernel(
     nb, nz, hours, freq_ref, owner_ref, loads_hbm, pair_hbm, share_hbm, out_ref,
-    loads_v, pair_v, share_v, sel_v, grid_v, spec_v,
-    rs_stage, rs_recv, bs_all, wall_stage, wall_recv, a_stage, a_recv,
+    loads_v, pair_v, share_v, sel_v, grid_v, cross_stage, cross_recv, spec_v,
+    rs_stage, rs_recv, bs_stage, bs_all, wall_stage, wall_recv,
     loads_sem, pair_sem, own_sem, sh_send, sh_recv, fw_send, fw_recv,
-    rs_ssem, rs_rsem, bs_ssem, bs_rsem, wl_ssem, wl_rsem, a_ssem, a_rsem,
+    cr_ssem, cr_rsem, rs_ssem, rs_rsem, bs_ssem, bs_rsem, wl_ssem, wl_rsem,
 ):
     b = lax.axis_index("bore")
     z = lax.axis_index("freq")
@@ -60,17 +60,19 @@
     freqs = freq_ref.shape[0]
     bores = owner_ref.shape[1]
     bloc = pair_hbm.shape[2]
+    scenarios = share_hbm.shape[0]
     s4 = sloc // nz
     core = b % 2
     chip = b // 2
     chips = nb // 2
     sibling = b + 1 - 2 * core
+    near_first = sorted(
+        ((r, k) for r in range(nb) for k in range(nz) if r or k), key=lambda rk: min(rk[1], nz - rk[1])
+    )
 
     barrier = pltpu.get_barrier_semaphore()
-    for r in range(1, nb):
-        pl.semaphore_signal(barrier, inc=1, device_id=((b + r) % nb, z), device_id_type=MESH)
-    for r in range(1, nz):
-        pl.semaphore_signal(barrier, inc=1, device_id=(b, (z + r) % nz), device_id_type=MESH)
+    for r, k in near_first:
+        pl.semaphore_signal(barrier, inc=1, device_id=((b + r) % nb, (z + k) % nz), device_id_type=MESH)
 
     parts = loads_sem.shape[0]
     sp = sloc // parts
@@ -82,9 +84,10 @@
         copy.start()
     own_share = pltpu.make_async_copy(share_hbm, share_v.at[b], own_sem)
     own_share.start()
+    turns = (1 - core, core)
     pair_copies = [
-        pltpu.make_async_copy(pair_hbm.at[f, d], pair_v.at[f, d], pair_sem.at[f, d])
-        for f in range(FLOC)
+        pltpu.make_async_copy(pair_hbm.at[turns[i], d], pair_v.at[turns[i], d], pair_sem.at[i, d])
+        for i in range(FLOC)
         for d in range(2)
     ]
 
@@ -95,7 +98,7 @@
     same = (to % freqs == part % freqs) & (to // freqs == part // (2 * freqs))
     join = jnp.where(same, jnp.where(to < freqs, 1.0, -1.0), 0.0).astype(jnp.bfloat16)
 
-    pl.semaphore_wait(barrier, nb - 1 + nz - 1)
+    pl.semaphore_wait(barrier, nb * nz - 1)
 
     share_copies = []
     for r in range(1, chips):
@@ -134,19 +137,18 @@
     )
     fold_from = lax.broadcasted_iota(jnp.int32, (lanes, 128), 0) % NBLD
     fold_to = lax.broadcasted_iota(jnp.int32, (lanes, 128), 1)
-    folded = jnp.zeros((nz * 2 * sloc, 128), jnp.float32)
-    for f in range(FLOC):
+    folded = jnp.zeros((freqs * sloc, 128), jnp.float32)
+    for c in range(2):
         spread = jnp.concatenate(
             [
-                jnp.where(keep, spec_v[pl.ds(c * freqs + k * FLOC + f, 1), :], 0.0).astype(jnp.bfloat16)
-                for k in range(nz)
-                for c in range(2)
+                jnp.where(keep, spec_v[pl.ds(c * freqs + k, 1), :], 0.0).astype(jnp.bfloat16)
+                for k in range(freqs)
             ],
             0,
         )
-        fold = (fold_from + f * NBLD == fold_to).astype(jnp.float32).astype(jnp.bfloat16)
+        fold = (fold_from + c * NBLD == fold_to).astype(jnp.float32).astype(jnp.bfloat16)
         folded = folded + jnp.dot(spread, fold, preferred_element_type=jnp.float32)
-    rs_stage[...] = folded.astype(jnp.bfloat16).reshape(nz, 2 * sloc, 128)
+    rs_stage[...] = folded.astype(jnp.bfloat16).reshape(nz, FLOC * sloc, 128)
 
     rs_copies = []
     for r in range(1, nz):
@@ -168,32 +170,56 @@
     here = sel_v[0:NBLD, pl.ds(pl.multiple_of(b * bloc, 128), bloc)]
     width = 1024
 
-    def gather_rows(f):
-        for d in range(2):
-            pair_copies[2 * f + d].wait()
-
-            def step(i, carry):
-                piece = pl.ds(pl.multiple_of(i * width, width), width)
-                total = jnp.dot(here, pair_v[f, d, :, piece], preferred_element_type=jnp.float32)
-                grid_v[f, pl.ds(d * NBLD, NBLD), piece] = total.astype(jnp.bfloat16)
-                return carry
-
-            lax.fori_loop(0, bores // width, step, 0)
-
-    gather_rows(0)
+    cross_copies = []
+
+    def gather_away(d):
+        pair_copies[d].wait()
+
+        def step(i, carry):
+            piece = pl.ds(pl.multiple_of(i * width, width), width)
+            total = jnp.dot(here, pair_v[turns[0], d, :, piece], preferred_element_type=jnp.float32)
+            cross_stage[d, :, piece] = total.astype(jnp.bfloat16)
+            return carry
+
+        lax.fori_loop(0, bores // width, step, 0)
+        cross_copies.append(
+            pltpu.make_async_remote_copy(
+                src_ref=cross_stage.at[d], dst_ref=cross_recv.at[d], send_sem=cr_ssem.at[d], recv_sem=cr_rsem.at[d],
+                device_id=(sibling, z), device_id_type=MESH,
+            )
+        )
+        cross_copies[-1].start()
+
+    def gather_here(d):
+        pair_copies[2 + d].wait()
+        cross_copies[d].wait_recv()
+
+        def step(i, carry):
+            piece = pl.ds(pl.multiple_of(i * width, width), width)
+            total = jnp.dot(here, pair_v[turns[1], d, :, piece], preferred_element_type=jnp.float32)
+            total = total + cross_recv[d, :, piece].astype(jnp.float32)
+            grid_v[pl.ds(d * NBLD, NBLD), piece] = total.astype(jnp.bfloat16)
+            return carry
+
+        lax.fori_loop(0, bores // width, step, 0)
+
+    gather_away(0)
+    gather_away(1)
 
     for copy in rs_copies:
         copy.wait_recv()
     spec = rs_recv[0].astype(jnp.float32)
     for k in range(1, nz):
         spec = spec + rs_recv[k].astype(jnp.float32)
-    bs_all[b] = spec.astype(jnp.bfloat16)
+    bs_stage[...] = spec.astype(jnp.bfloat16).reshape(FLOC, sloc, 128)
+    bs_all[b] = bs_stage[core]
     bs_copies = []
     for r in range(1, nb):
+        to = (b + r) % nb
         bs_copies.append(
             pltpu.make_async_remote_copy(
-                src_ref=bs_all.at[b], dst_ref=bs_all.at[b], send_sem=bs_ssem.at[r], recv_sem=bs_rsem.at[r],
-                device_id=((b + r) % nb, z), device_id_type=MESH,
+                src_ref=bs_stage.at[to % 2], dst_ref=bs_all.at[b], send_sem=bs_ssem.at[r], recv_sem=bs_rsem.at[r],
+                device_id=(to, z), device_id_type=MESH,
             )
         )
         bs_copies[-1].start()
@@ -210,79 +236,53 @@
         )
         fw_copies[-1].start()
 
-    gather_rows(1)
+    gather_here(0)
+    gather_here(1)
 
     own_share.wait()
     share_copies[-1].wait_recv()
+    for copy in fw_copies:
+        copy.wait_recv()
     for copy in bs_copies:
         copy.wait_recv()
-    for copy in fw_copies:
-        copy.wait_recv()
-
-    rows = nb * 2 * sloc
-    spec_all = bs_all[...].reshape(rows, 128).astype(jnp.float32)
-    half = lax.broadcasted_iota(jnp.int32, (rows, 128), 1) // NBLD
-    spec_f = [jnp.where(half == f, spec_all, 0.0).astype(jnp.bfloat16) for f in range(FLOC)]
+
+    spec_all = bs_all[...].reshape(scenarios, 128).astype(jnp.float32)
+    half = lax.broadcasted_iota(jnp.int32, (scenarios, 128), 1) // NBLD
+    spec_c = jnp.concatenate([jnp.where(half == c, spec_all, 0.0).astype(jnp.bfloat16) for c in range(2)], 0)
 
     def source_step(q, walls):
         piece = pl.ds(pl.multiple_of(q * bloc, 128), bloc)
-        select = sel_v[:, piece]
-        weight = share_v[q].astype(jnp.float32).reshape(nb, 1, sloc, bloc)
-        new = []
-        for f in range(FLOC):
-            picked = jnp.dot(spec_f[f], select, preferred_element_type=jnp.float32)
-            source = (picked.reshape(nb, 2, sloc, bloc) * weight).astype(jnp.bfloat16).reshape(rows, bloc)
-            new.append(
-                walls[f] + lax.dot_general(source, grid_v[f, :, piece], NT, preferred_element_type=jnp.float32)
-            )
-        return tuple(new)
-
-    walls = lax.fori_loop(0, nb, source_step, tuple(jnp.zeros((rows, 128), jnp.float32) for _ in range(FLOC)), unroll=8)
-    sign = jnp.where(lax.broadcasted_iota(jnp.int32, (nb * sloc, 128), 1) < NBLD, -1.0, 1.0)
-    for f in range(FLOC):
-        crossed = walls[f].reshape(nb, 2, sloc, 128)
-        real = crossed[:, 0].reshape(nb * sloc, 128)
-        imag = crossed[:, 1].reshape(nb * sloc, 128)
-        joined = real + sign * pltpu.roll(imag, NBLD, 1)
-        wall_stage[:, f] = joined.astype(jnp.bfloat16).reshape(nb, sloc, 128)
-
+        weight = share_v[q].astype(jnp.float32)
+        picked = jnp.dot(spec_c, sel_v[:, piece], preferred_element_type=jnp.float32)
+        source = (picked.reshape(2, scenarios, bloc) * weight).astype(jnp.bfloat16).reshape(2 * scenarios, bloc)
+        return walls + lax.dot_general(source, grid_v[:, piece], NT, preferred_element_type=jnp.float32)
+
+    walls = lax.fori_loop(0, nb, source_step, jnp.zeros((2 * scenarios, 128), jnp.float32), unroll=8)
+    sign = jnp.where(lax.broadcasted_iota(jnp.int32, (scenarios, 128), 1) < NBLD, -1.0, 1.0)
+    joined = (walls[:scenarios] + sign * pltpu.roll(walls[scenarios:], NBLD, 1)) * (NBLD / bores)
+    wall_stage[...] = joined.reshape(nb * nz, s4, 128)
+
+    slot = z * FLOC + core
     wl_copies = []
-    for r in range(1, nb):
-        to = (b + r) % nb
+    for r, k in near_first[::-1]:
+        to_b, to_z = (b + r) % nb, (z + k) % nz
         wl_copies.append(
             pltpu.make_async_remote_copy(
-                src_ref=wall_stage.at[to], dst_ref=wall_recv.at[b], send_sem=wl_ssem.at[r], recv_sem=wl_rsem.at[r],
-                device_id=(to, z), device_id_type=MESH,
+                src_ref=wall_stage.at[to_b * nz + to_z], dst_ref=wall_recv.at[slot, chip],
+                send_sem=wl_ssem.at[r, k], recv_sem=wl_rsem.at[r, k],
+                device_id=(to_b, to_z), device_id_type=MESH,
             )
         )
         wl_copies[-1].start()
-    wall_recv[b] = wall_stage[b]
+    wall_recv[slot, chip] = wall_stage[b * nz + z]
+    for copy in share_copies + rs_copies + bs_copies + fw_copies + cross_copies:
+        copy.wait_send()
     for copy in wl_copies:
-        copy.wait_recv()
-    wall = wall_recv[0].astype(jnp.float32)
-    for q in range(1, nb):
-        wall = wall + wall_recv[q].astype(jnp.float32)
-    wall = wall * (NBLD / bores)
-    for k in range(nz):
-        for f in range(FLOC):
-            a_stage[k, f * s4 : (f + 1) * s4, :] = wall[f, k * s4 : (k + 1) * s4, :]
-
-    a_copies = []
-    for r in range(1, nz):
-        to = (z + r) % nz
-        a_copies.append(
-            pltpu.make_async_remote_copy(
-                src_ref=a_stage.at[to], dst_ref=a_recv.at[z], send_sem=a_ssem.at[r], recv_sem=a_rsem.at[r],
-                device_id=(b, to), device_id_type=MESH,
-            )
-        )
-        a_copies[-1].start()
-    a_recv[z] = a_stage[z]
-    for copy in share_copies + rs_copies + bs_copies + fw_copies + wl_copies:
-        copy.wait_send()
-    for copy in a_copies:
         copy.wait()
-    out_ref[...] = a_recv[...].reshape(nz * FLOC * s4, 128)
+    wall = wall_recv[:, 0]
+    for q in range(1, chips):
+        wall = wall + wall_recv[:, q]
+    out_ref[...] = wall.reshape(freqs * s4, 128)
 
 
 def superpose(loads, pair_spectra, share, owners, freq_index, nb, nz):
@@ -309,15 +309,16 @@
             pltpu.VMEM(pair_spectra.shape, bf16),
             pltpu.VMEM((nb, scenarios, bloc), bf16),
             pltpu.VMEM((2 * NBLD, bores), bf16),
-            pltpu.VMEM((FLOC, 2 * NBLD, bores), bf16),
+            pltpu.VMEM((2 * NBLD, bores), bf16),
+            pltpu.VMEM((2, NBLD, bores), bf16),
+            pltpu.VMEM((2, NBLD, bores), bf16),
             pltpu.VMEM((2 * freqs, sloc * NBLD), f32),
-            pltpu.VMEM((nz, 2 * sloc, 128), bf16),
-            pltpu.VMEM((nz, 2 * sloc, 128), bf16),
-            pltpu.VMEM((nb, 2 * sloc, 128), bf16),
-            pltpu.VMEM((nb, FLOC, sloc, 128), bf16),
-            pltpu.VMEM((nb, FLOC, sloc, 128), bf16),
-            pltpu.VMEM((nz, FLOC * s4, 128), f32),
-            pltpu.VMEM((nz, FLOC * s4, 128), f32),
+            pltpu.VMEM((nz, FLOC * sloc, 128), bf16),
+            pltpu.VMEM((nz, FLOC * sloc, 128), bf16),
+            pltpu.VMEM((FLOC, sloc, 128), bf16),
+            pltpu.VMEM((nb, sloc, 128), bf16),
+            pltpu.VMEM((nb * nz, s4, 128), f32),
+            pltpu.VMEM((freqs, nb // 2, s4, 128), f32),
             dma((4,)),
             dma((FLOC, 2)),
             dma,
@@ -325,14 +326,14 @@
             dma((nb // 2,)),
             dma((nb // 2,)),
             dma((nb // 2,)),
+            dma((2,)),
+            dma((2,)),
             dma((nz,)),
             dma((nz,)),
             dma((nb,)),
             dma((nb,)),
-            dma((nb,)),
-            dma((nb,)),
-            dma((nz,)),
-            dma((nz,)),
+            dma((nb, nz)),
+            dma((nb, nz)),
         ],
         compiler_params=pltpu.CompilerParams(
             collective_id=0, has_side_effects=True, vmem_limit_bytes=56 * 2**20

time: 30.3 us -> 29.1 us (0.960)
  Pallas kernels: 30 us -> 28.8 us
    pallas_call x1, Pallas kernels: 26.8 us -> 25.6 us  [superpose(): pl.pallas_call(functools.partial(superpose_kernel, nb, nz, tloc * nz), ou...]
where the time goes in v2:
time: 29.1 us; the launch traced here: 28.8 us
  Pallas kernels  28.8 us (99%)
    pallas_call x1, Pallas kernels, superpose(): pl.pallas_call(functools.partial(superpose_kernel, nb, nz, tloc * nz), ou...  25.6 us
    pallas_call x1, Pallas kernels, inverse(): pl.pallas_call(functools.partial(inverse_kernel, hours), out_shape=jax.Sh...  3.2 us

profile of v2, /device:TPU:0, one launch (start us, length us, event | category | flops | bytes accessed | tf_op | source)
XLA Modules:
  0.0 28.8 jit_solution(10016250406084794676)
XLA Ops:
  0.0 25.6 %superpose.1.wall_v = f32[32,128]{1,0:T(8,128)S(1)} custom-call(s32[8]{0:T(128)} %freq_ref.3, s32[1,4096]{1,0:T(1,128)} %bitcast.1, bf16[16,64,2048]{2,1,0:T(8,128)(2,1)} %loads_hbm.1, bf16[2,2,512,4096]{3,2,1,0:T(8,128)(2,1)} %pair_hbm.1, bf16[128,512]{1,0:T(8,128)(2,1)} %share_hbm.1), custom_call_target="tpu_custom_call" | custom-call | tf_op jit(solution)/shard_map/superpose/pallas_call | solution.py:296
  25.6 3.2 %inverse.1 = bf16[4,64,8192]{2,1,0:T(8,128)(2,1)} custom-call(s32[8]{0:T(128)} %freq_ref.3, f32[32,128]{1,0:T(8,128)S(1)} %superpose.1.wall_v), custom_call_target="tpu_custom_call" | custom-call | tf_op jit(solution)/shard_map/inverse/pallas_call | solution.py:385

commit v3 on v2

--- a/solution.py
+++ b/solution.py
@@ -48,7 +48,7 @@
 
 def superpose_kernel(
     nb, nz, hours, freq_ref, owner_ref, loads_hbm, pair_hbm, share_hbm, out_ref,
-    loads_v, pair_v, share_v, sel_v, grid_v, cross_stage, cross_recv, spec_v,
+    loads_v, pair_v, share_v, sel_v, grid_v, cross_stage, cross_recv,
     rs_stage, rs_recv, bs_stage, bs_all, wall_stage, wall_recv,
     loads_sem, pair_sem, own_sem, sh_send, sh_recv, fw_send, fw_recv,
     cr_ssem, cr_rsem, rs_ssem, rs_rsem, bs_ssem, bs_rsem, wl_ssem, wl_rsem,
@@ -74,13 +74,20 @@
     for r, k in near_first:
         pl.semaphore_signal(barrier, inc=1, device_id=((b + r) % nb, (z + k) % nz), device_id_type=MESH)
 
-    parts = loads_sem.shape[0]
-    sp = sloc // parts
+    sp = sloc // 2
+    hp = tloc // 2
     load_copies = [
-        pltpu.make_async_copy(loads_hbm.at[pl.ds(i * sp, sp)], loads_v.at[pl.ds(i * sp, sp)], loads_sem.at[i])
-        for i in range(parts)
+        [
+            pltpu.make_async_copy(
+                loads_hbm.at[pl.ds(i * sp, sp), :, pl.ds(h * hp, hp)],
+                loads_v.at[pl.ds(i * sp, sp), :, pl.ds(h * hp, hp)],
+                loads_sem.at[i, h],
+            )
+            for h in range(2)
+        ]
+        for i in range(2)
     ]
-    for copy in load_copies:
+    for copy in load_copies[0] + load_copies[1]:
         copy.start()
     own_share = pltpu.make_async_copy(share_hbm, share_v.at[b], own_sem)
     own_share.start()
@@ -93,10 +100,11 @@
 
     cos, sin = cos_sin(harmonic_column(freq_ref, freqs), z * tloc, tloc, hours)
     table = jnp.concatenate([*halves(cos), *halves(sin)], 0)
-    to = lax.broadcasted_iota(jnp.int32, (2 * freqs, 4 * freqs), 0)
-    part = lax.broadcasted_iota(jnp.int32, (2 * freqs, 4 * freqs), 1)
-    same = (to % freqs == part % freqs) & (to // freqs == part // (2 * freqs))
-    join = jnp.where(same, jnp.where(to < freqs, 1.0, -1.0), 0.0).astype(jnp.bfloat16)
+    lanes = sp * NBLD
+    keep = lax.broadcasted_iota(jnp.int32, (sp, lanes), 1) // NBLD == lax.broadcasted_iota(jnp.int32, (sp, lanes), 0)
+    fold_from = lax.broadcasted_iota(jnp.int32, (lanes, 128), 0) % NBLD
+    fold_to = lax.broadcasted_iota(jnp.int32, (lanes, 128), 1)
+    folds = [(fold_from + c * NBLD == fold_to).astype(jnp.float32).astype(jnp.bfloat16) for c in range(2)]
 
     pl.semaphore_wait(barrier, nb * nz - 1)
 
@@ -117,38 +125,26 @@
     for copy in share_copies:
         copy.start()
 
-    for i, copy in enumerate(load_copies):
-        copy.wait()
-        if i < len(pair_copies):
-            pair_copies[i].start()
-        chunk = loads_v[pl.ds(i * sp, sp)].reshape(sp * NBLD, tloc)
-        x = lax.dot_general(chunk, table, NT, preferred_element_type=jnp.float32)
-        upper, lower = halves(x)
-        spec_v[:, pl.ds(i * sp * NBLD, sp * NBLD)] = (
-            lax.dot_general(join, upper, NT, preferred_element_type=jnp.float32)
-            + lax.dot_general(join, lower, NT, preferred_element_type=jnp.float32)
-        ) * (1.0 / math.sqrt(hours))
-    for copy in pair_copies[parts:]:
-        copy.start()
-
-    lanes = sloc * NBLD
-    keep = lax.broadcasted_iota(jnp.int32, (sloc, lanes), 1) // NBLD == lax.broadcasted_iota(
-        jnp.int32, (sloc, lanes), 0
-    )
-    fold_from = lax.broadcasted_iota(jnp.int32, (lanes, 128), 0) % NBLD
-    fold_to = lax.broadcasted_iota(jnp.int32, (lanes, 128), 1)
-    folded = jnp.zeros((freqs * sloc, 128), jnp.float32)
-    for c in range(2):
-        spread = jnp.concatenate(
-            [
-                jnp.where(keep, spec_v[pl.ds(c * freqs + k, 1), :], 0.0).astype(jnp.bfloat16)
-                for k in range(freqs)
-            ],
-            0,
-        )
-        fold = (fold_from + c * NBLD == fold_to).astype(jnp.float32).astype(jnp.bfloat16)
-        folded = folded + jnp.dot(spread, fold, preferred_element_type=jnp.float32)
-    rs_stage[...] = folded.astype(jnp.bfloat16).reshape(nz, FLOC * sloc, 128)
+    folded = []
+    for i in range(2):
+        spec = jnp.zeros((4 * freqs, lanes), jnp.float32)
+        for h in range(2):
+            load_copies[i][h].wait()
+            pair_copies[2 * i + h].start()
+            chunk = loads_v[pl.ds(i * sp, sp), :, pl.ds(h * hp, hp)].reshape(lanes, hp)
+            spec = spec + lax.dot_general(
+                table[:, h * hp : (h + 1) * hp], chunk, NT, preferred_element_type=jnp.float32
+            )
+        total = jnp.zeros((freqs * sp, 128), jnp.float32)
+        for c in range(2):
+            upper, lower = spec[2 * c * freqs : (2 * c + 1) * freqs], spec[(2 * c + 1) * freqs : (2 * c + 2) * freqs]
+            part = (upper + lower) * ((1.0 - 2.0 * c) / math.sqrt(hours))
+            spread = jnp.concatenate(
+                [jnp.where(keep, part[k : k + 1], 0.0).astype(jnp.bfloat16) for k in range(freqs)], 0
+            )
+            total = total + jnp.dot(spread, folds[c], preferred_element_type=jnp.float32)
+        folded.append(total.reshape(freqs, sp, 128))
+    rs_stage[...] = jnp.concatenate(folded, 1).astype(jnp.bfloat16).reshape(nz, FLOC * sloc, 128)
 
     rs_copies = []
     for r in range(1, nz):
@@ -312,14 +308,13 @@
             pltpu.VMEM((2 * NBLD, bores), bf16),
             pltpu.VMEM((2, NBLD, bores), bf16),
             pltpu.VMEM((2, NBLD, bores), bf16),
-            pltpu.VMEM((2 * freqs, sloc * NBLD), f32),
             pltpu.VMEM((nz, FLOC * sloc, 128), bf16),
             pltpu.VMEM((nz, FLOC * sloc, 128), bf16),
             pltpu.VMEM((FLOC, sloc, 128), bf16),
             pltpu.VMEM((nb, sloc, 128), bf16),
             pltpu.VMEM((nb * nz, s4, 128), f32),
             pltpu.VMEM((freqs, nb // 2, s4, 128), f32),
-            dma((4,)),
+            dma((2, 2)),
             dma((FLOC, 2)),
             dma,
             dma((nb // 2,)),

time: 29.1 us -> 28.2 us (0.969)
  Pallas kernels: 28.8 us -> 28 us
    pallas_call x1, Pallas kernels: 25.6 us -> 24.8 us  [superpose(): pl.pallas_call(functools.partial(superpose_kernel, nb, nz, tloc * nz), ou...]
where the time goes in v3:
time: 28.2 us; the launch traced here: 28 us
  Pallas kernels  28 us (99%)
    pallas_call x1, Pallas kernels, superpose(): pl.pallas_call(functools.partial(superpose_kernel, nb, nz, tloc * nz), ou...  24.8 us
    pallas_call x1, Pallas kernels, inverse(): pl.pallas_call(functools.partial(inverse_kernel, hours), out_shape=jax.Sh...  3.18 us

profile of v3, /device:TPU:0, one launch (start us, length us, event | category | flops | bytes accessed | tf_op | source)
XLA Modules:
  0.0 28.0 jit_solution(15304935599098145579)
XLA Ops:
  0.0 24.8 %superpose.1.wall_v = f32[32,128]{1,0:T(8,128)S(1)} custom-call(s32[8]{0:T(128)} %freq_ref.3, s32[1,4096]{1,0:T(1,128)} %bitcast.1, bf16[16,64,2048]{2,1,0:T(8,128)(2,1)} %loads_hbm.1, bf16[2,2,512,4096]{3,2,1,0:T(8,128)(2,1)} %pair_hbm.1, bf16[128,512]{1,0:T(8,128)(2,1)} %share_hbm.1), custom_call_target="tpu_custom_call" | custom-call | tf_op jit(solution)/shard_map/superpose/pallas_call | solution.py:292
  24.8 3.2 %inverse.1 = bf16[4,64,8192]{2,1,0:T(8,128)(2,1)} custom-call(s32[8]{0:T(128)} %freq_ref.3, f32[32,128]{1,0:T(8,128)S(1)} %superpose.1.wall_v), custom_call_target="tpu_custom_call" | custom-call | tf_op jit(solution)/shard_map/inverse/pallas_call | solution.py:380

commit v4 on v3

--- a/solution.py
+++ b/solution.py
@@ -49,9 +49,9 @@
 def superpose_kernel(
     nb, nz, hours, freq_ref, owner_ref, loads_hbm, pair_hbm, share_hbm, out_ref,
     loads_v, pair_v, share_v, sel_v, grid_v, cross_stage, cross_recv,
-    rs_stage, rs_recv, bs_stage, bs_all, wall_stage, wall_recv,
+    bs_stage, bs_all, wall_stage, wall_recv,
     loads_sem, pair_sem, own_sem, sh_send, sh_recv, fw_send, fw_recv,
-    cr_ssem, cr_rsem, rs_ssem, rs_rsem, bs_ssem, bs_rsem, wl_ssem, wl_rsem,
+    cr_ssem, cr_rsem, bs_ssem, bs_rsem, wl_ssem, wl_rsem,
 ):
     b = lax.axis_index("bore")
     z = lax.axis_index("freq")
@@ -70,10 +70,8 @@
         ((r, k) for r in range(nb) for k in range(nz) if r or k), key=lambda rk: min(rk[1], nz - rk[1])
     )
 
-    barrier = pltpu.get_barrier_semaphore()
-    for r, k in near_first:
-        pl.semaphore_signal(barrier, inc=1, device_id=((b + r) % nb, (z + k) % nz), device_id_type=MESH)
-
+    own_share = pltpu.make_async_copy(share_hbm, share_v.at[b], own_sem)
+    own_share.start()
     sp = sloc // 2
     hp = tloc // 2
     load_copies = [
@@ -89,8 +87,10 @@
     ]
     for copy in load_copies[0] + load_copies[1]:
         copy.start()
-    own_share = pltpu.make_async_copy(share_hbm, share_v.at[b], own_sem)
-    own_share.start()
+    barrier = pltpu.get_barrier_semaphore()
+    for r, k in near_first:
+        pl.semaphore_signal(barrier, inc=1, device_id=((b + r) % nb, (z + k) % nz), device_id_type=MESH)
+
     turns = (1 - core, core)
     pair_copies = [
         pltpu.make_async_copy(pair_hbm.at[turns[i], d], pair_v.at[turns[i], d], pair_sem.at[i, d])
@@ -106,22 +106,26 @@
     fold_to = lax.broadcasted_iota(jnp.int32, (lanes, 128), 1)
     folds = [(fold_from + c * NBLD == fold_to).astype(jnp.float32).astype(jnp.bfloat16) for c in range(2)]
 
+    square = chips == 4
+    over_x = chip + 1 - 2 * (chip % 2)
+    over_y = (chip + 2) % chips
+    first_hops = (over_x, over_y) if square else tuple((chip + r) % chips for r in range(1, chips))
+    first_from = first_hops if square else tuple((chip + chips - r) % chips for r in range(1, chips))
+    share_copies = [
+        pltpu.make_async_remote_copy(
+            src_ref=share_v.at[b], dst_ref=share_v.at[b], send_sem=sh_send.at[r], recv_sem=sh_recv.at[r],
+            device_id=device, device_id_type=MESH,
+        )
+        for r, device in enumerate([(to * 2 + core, z) for to in first_hops] + [(sibling, z)])
+    ]
+
+    for q in range(nb):
+        piece = pl.ds(q * bloc, bloc)
+        label = lax.broadcasted_iota(jnp.int32, (2 * NBLD, bloc), 0) % NBLD
+        sel_v[:, piece] = (label == owner_ref[:, piece]).astype(jnp.float32).astype(jnp.bfloat16)
+
     pl.semaphore_wait(barrier, nb * nz - 1)
-
-    share_copies = []
-    for r in range(1, chips):
-        share_copies.append(
-            pltpu.make_async_remote_copy(
-                src_ref=share_hbm, dst_ref=share_v.at[b], send_sem=sh_send.at[r], recv_sem=sh_recv.at[r],
-                device_id=((chip + r) % chips * 2 + core, z), device_id_type=MESH,
-            )
-        )
-    share_copies.append(
-        pltpu.make_async_remote_copy(
-            src_ref=share_hbm, dst_ref=share_v.at[b], send_sem=sh_send.at[0], recv_sem=sh_recv.at[0],
-            device_id=(sibling, z), device_id_type=MESH,
-        )
-    )
+    own_share.wait()
     for copy in share_copies:
         copy.start()
 
@@ -144,27 +148,35 @@
             )
             total = total + jnp.dot(spread, folds[c], preferred_element_type=jnp.float32)
         folded.append(total.reshape(freqs, sp, 128))
-    rs_stage[...] = jnp.concatenate(folded, 1).astype(jnp.bfloat16).reshape(nz, FLOC * sloc, 128)
-
-    rs_copies = []
-    for r in range(1, nz):
-        to = (z + r) % nz
-        rs_copies.append(
+    bs_stage[...] = jnp.concatenate(folded, 1).astype(jnp.bfloat16)
+
+    bs_copies = []
+    for r, k in near_first[::-1]:
+        to_b, to_z = (b + r) % nb, (z + k) % nz
+        bs_copies.append(
             pltpu.make_async_remote_copy(
-                src_ref=rs_stage.at[to], dst_ref=rs_recv.at[z], send_sem=rs_ssem.at[r], recv_sem=rs_rsem.at[r],
-                device_id=(b, to), device_id_type=MESH,
+                src_ref=bs_stage.at[to_z * FLOC + to_b % 2], dst_ref=bs_all.at[z, b],
+                send_sem=bs_ssem.at[r, k], recv_sem=bs_rsem.at[r, k],
+                device_id=(to_b, to_z), device_id_type=MESH,
             )
         )
-        rs_copies[-1].start()
-    rs_recv[z] = rs_stage[z]
-
-    for q in range(nb):
-        piece = pl.ds(q * bloc, bloc)
-        label = lax.broadcasted_iota(jnp.int32, (2 * NBLD, bloc), 0) % NBLD
-        sel_v[:, piece] = (label == owner_ref[:, piece]).astype(jnp.float32).astype(jnp.bfloat16)
+        bs_copies[-1].start()
+    bs_all[z, b] = bs_stage[z * FLOC + core]
+
+    fw_copies = []
+
+    def forward(r, origin, rows, device):
+        there = share_v.at[origin, rows]
+        fw_copies.append(
+            pltpu.make_async_remote_copy(
+                src_ref=there, dst_ref=there, send_sem=fw_send.at[r], recv_sem=fw_recv.at[r],
+                device_id=(device, z), device_id_type=MESH,
+            )
+        )
+        fw_copies[-1].start()
 
     here = sel_v[0:NBLD, pl.ds(pl.multiple_of(b * bloc, 128), bloc)]
-    width = 1024
+    width = 2048
 
     cross_copies = []
 
@@ -202,79 +214,78 @@
     gather_away(0)
     gather_away(1)
 
-    for copy in rs_copies:
-        copy.wait_recv()
-    spec = rs_recv[0].astype(jnp.float32)
-    for k in range(1, nz):
-        spec = spec + rs_recv[k].astype(jnp.float32)
-    bs_stage[...] = spec.astype(jnp.bfloat16).reshape(FLOC, sloc, 128)
-    bs_all[b] = bs_stage[core]
-    bs_copies = []
-    for r in range(1, nb):
-        to = (b + r) % nb
-        bs_copies.append(
-            pltpu.make_async_remote_copy(
-                src_ref=bs_stage.at[to % 2], dst_ref=bs_all.at[b], send_sem=bs_ssem.at[r], recv_sem=bs_rsem.at[r],
-                device_id=(to, z), device_id_type=MESH,
-            )
-        )
-        bs_copies[-1].start()
-
-    fw_copies = []
-    for r in range(1, chips):
-        share_copies[r - 1].wait_recv()
-        origin = (chip + chips - r) % chips * 2 + core
-        fw_copies.append(
-            pltpu.make_async_remote_copy(
-                src_ref=share_v.at[origin], dst_ref=share_v.at[origin], send_sem=fw_send.at[r], recv_sem=fw_recv.at[r],
-                device_id=(sibling, z), device_id_type=MESH,
-            )
-        )
-        fw_copies[-1].start()
+    every = slice(0, scenarios)
+    for r, origin in enumerate(first_from):
+        share_copies[r].wait_recv()
+        if square:
+            rows = pl.ds(r * (scenarios // 2), scenarios // 2)
+            forward(chips + r, origin * 2 + core, rows, first_hops[1 - r] * 2 + core)
+        forward(r, origin * 2 + core, every, sibling)
+
 
     gather_here(0)
     gather_here(1)
 
-    own_share.wait()
+    if square:
+        for r in range(2):
+            fw_copies[2 * r].wait_recv()
+        forward(2, (over_x + 2) % chips * 2 + core, every, sibling)
+
     share_copies[-1].wait_recv()
-    for copy in fw_copies:
+    for copy in (fw_copies[1], fw_copies[3]) if square else fw_copies:
         copy.wait_recv()
     for copy in bs_copies:
         copy.wait_recv()
 
-    spec_all = bs_all[...].reshape(scenarios, 128).astype(jnp.float32)
+    spec_all = bs_all[0].astype(jnp.float32)
+    for k in range(1, nz):
+        spec_all = spec_all + bs_all[k].astype(jnp.float32)
+    spec_all = spec_all.reshape(scenarios, 128)
     half = lax.broadcasted_iota(jnp.int32, (scenarios, 128), 1) // NBLD
     spec_c = jnp.concatenate([jnp.where(half == c, spec_all, 0.0).astype(jnp.bfloat16) for c in range(2)], 0)
 
-    def source_step(q, walls):
-        piece = pl.ds(pl.multiple_of(q * bloc, 128), bloc)
-        weight = share_v[q].astype(jnp.float32)
-        picked = jnp.dot(spec_c, sel_v[:, piece], preferred_element_type=jnp.float32)
-        source = (picked.reshape(2, scenarios, bloc) * weight).astype(jnp.bfloat16).reshape(2 * scenarios, bloc)
-        return walls + lax.dot_general(source, grid_v[:, piece], NT, preferred_element_type=jnp.float32)
-
-    walls = lax.fori_loop(0, nb, source_step, jnp.zeros((2 * scenarios, 128), jnp.float32), unroll=8)
+    def source_blocks(origins, walls):
+        for q in origins:
+            piece = pl.ds(pl.multiple_of(q * bloc, 128), bloc)
+            weight = share_v[q].astype(jnp.float32)
+            picked = jnp.dot(spec_c, sel_v[:, piece], preferred_element_type=jnp.float32)
+            source = (picked.reshape(2, scenarios, bloc) * weight).astype(jnp.bfloat16).reshape(2 * scenarios, bloc)
+            walls = walls + lax.dot_general(source, grid_v[:, piece], NT, preferred_element_type=jnp.float32)
+        return walls
+
+    walls = jnp.zeros((2 * scenarios, 128), jnp.float32)
+    if square:
+        walls = source_blocks([q * 2 + c for q in (chip, over_x, over_y) for c in range(2)], walls)
+        fw_copies[4].wait_recv()
+        diagonal = (over_x + 2) % chips
+        walls = source_blocks([diagonal * 2 + c for c in range(2)], walls)
+    else:
+        walls = source_blocks(range(nb), walls)
     sign = jnp.where(lax.broadcasted_iota(jnp.int32, (scenarios, 128), 1) < NBLD, -1.0, 1.0)
     joined = (walls[:scenarios] + sign * pltpu.roll(walls[scenarios:], NBLD, 1)) * (NBLD / bores)
     wall_stage[...] = joined.reshape(nb * nz, s4, 128)
 
     slot = z * FLOC + core
-    wl_copies = []
-    for r, k in near_first[::-1]:
-        to_b, to_z = (b + r) % nb, (z + k) % nz
-        wl_copies.append(
-            pltpu.make_async_remote_copy(
-                src_ref=wall_stage.at[to_b * nz + to_z], dst_ref=wall_recv.at[slot, chip],
-                send_sem=wl_ssem.at[r, k], recv_sem=wl_rsem.at[r, k],
-                device_id=(to_b, to_z), device_id_type=MESH,
-            )
+    def wall_copy(r, to_z, from_z):
+        to_b = (b + r) % nb
+        return pltpu.make_async_remote_copy(
+            src_ref=wall_stage.at[to_b * nz + to_z], dst_ref=wall_recv.at[slot, chip],
+            send_sem=wl_ssem.at[r, to_z], recv_sem=wl_rsem.at[r, from_z],
+            device_id=(to_b, to_z), device_id_type=MESH,
         )
-        wl_copies[-1].start()
+
+    plane_first = []
+    for k in range(nz):
+        plane_first += [(r, k) for r in range(1, nb)]
+        if k < nz - 1:
+            plane_first.append((0, k + (z <= k).astype(jnp.int32)))
+    for r, k in plane_first:
+        wall_copy(r, k, z).start()
     wall_recv[slot, chip] = wall_stage[b * nz + z]
-    for copy in share_copies + rs_copies + bs_copies + fw_copies + cross_copies:
+    for copy in share_copies + bs_copies + fw_copies + cross_copies:
         copy.wait_send()
-    for copy in wl_copies:
-        copy.wait()
+    for r, k in plane_first:
+        wall_copy(r, k, k).wait()
     wall = wall_recv[:, 0]
     for q in range(1, chips):
         wall = wall + wall_recv[:, q]
@@ -308,10 +319,8 @@
             pltpu.VMEM((2 * NBLD, bores), bf16),
             pltpu.VMEM((2, NBLD, bores), bf16),
             pltpu.VMEM((2, NBLD, bores), bf16),
-            pltpu.VMEM((nz, FLOC * sloc, 128), bf16),
-            pltpu.VMEM((nz, FLOC * sloc, 128), bf16),
-            pltpu.VMEM((FLOC, sloc, 128), bf16),
-            pltpu.VMEM((nb, sloc, 128), bf16),
+            pltpu.VMEM((freqs, sloc, 128), bf16),
+            pltpu.VMEM((nz, nb, sloc, 128), bf16),
             pltpu.VMEM((nb * nz, s4, 128), f32),
             pltpu.VMEM((freqs, nb // 2, s4, 128), f32),
             dma((2, 2)),
@@ -319,14 +328,12 @@
             dma,
             dma((nb // 2,)),
             dma((nb // 2,)),
-            dma((nb // 2,)),
-            dma((nb // 2,)),
+            dma((nb // 2 + 2,)),
+            dma((nb // 2 + 2,)),
             dma((2,)),
             dma((2,)),
-            dma((nz,)),
-            dma((nz,)),
-            dma((nb,)),
-            dma((nb,)),
+            dma((nb, nz)),
+            dma((nb, nz)),
             dma((nb, nz)),
             dma((nb, nz)),
         ],

time: 28.2 us -> 26.8 us (0.950)
  Pallas kernels: 28 us -> 26.6 us
    pallas_call x1, Pallas kernels: 24.8 us -> 23.4 us  [superpose(): pl.pallas_call(functools.partial(superpose_kernel, nb, nz, tloc * nz), ou...]
where the time goes in v4:
time: 26.8 us; the launch traced here: 26.6 us
  Pallas kernels  26.6 us (99%)
    pallas_call x1, Pallas kernels, superpose(): pl.pallas_call(functools.partial(superpose_kernel, nb, nz, tloc * nz), ou...  23.4 us
    pallas_call x1, Pallas kernels, inverse(): pl.pallas_call(functools.partial(inverse_kernel, hours), out_shape=jax.Sh...  3.18 us

profile of v4, /device:TPU:0, one launch (start us, length us, event | category | flops | bytes accessed | tf_op | source)
XLA Modules:
  0.0 26.6 jit_solution(10800535643270617037)
XLA Ops:
  0.0 23.4 %superpose.1.wall_v = f32[32,128]{1,0:T(8,128)S(1)} custom-call(s32[8]{0:T(128)} %freq_ref.3, s32[1,4096]{1,0:T(1,128)} %bitcast.1, bf16[16,64,2048]{2,1,0:T(8,128)(2,1)} %loads_hbm.1, bf16[2,2,512,4096]{3,2,1,0:T(8,128)(2,1)} %pair_hbm.1, bf16[128,512]{1,0:T(8,128)(2,1)} %share_hbm.1), custom_call_target="tpu_custom_call" | custom-call | tf_op jit(solution)/shard_map/superpose/pallas_call | solution.py:303
  23.4 3.2 %inverse.1 = bf16[4,64,8192]{2,1,0:T(8,128)(2,1)} custom-call(s32[8]{0:T(128)} %freq_ref.3, f32[32,128]{1,0:T(8,128)S(1)} %superpose.1.wall_v), custom_call_target="tpu_custom_call" | custom-call | tf_op jit(solution)/shard_map/inverse/pallas_call | solution.py:387

commit v5 on v4

--- a/solution.py
+++ b/solution.py
@@ -226,11 +226,6 @@
     gather_here(0)
     gather_here(1)
 
-    if square:
-        for r in range(2):
-            fw_copies[2 * r].wait_recv()
-        forward(2, (over_x + 2) % chips * 2 + core, every, sibling)
-
     share_copies[-1].wait_recv()
     for copy in (fw_copies[1], fw_copies[3]) if square else fw_copies:
         copy.wait_recv()
@@ -255,10 +250,14 @@
 
     walls = jnp.zeros((2 * scenarios, 128), jnp.float32)
     if square:
-        walls = source_blocks([q * 2 + c for q in (chip, over_x, over_y) for c in range(2)], walls)
+        diagonal = (over_x + 2) % chips * 2
+        walls = source_blocks([b, sibling, over_x * 2, over_x * 2 + 1], walls)
+        for r in range(2):
+            fw_copies[2 * r].wait_recv()
+        forward(2, diagonal + core, every, sibling)
+        walls = source_blocks([over_y * 2, over_y * 2 + 1, diagonal + core], walls)
         fw_copies[4].wait_recv()
-        diagonal = (over_x + 2) % chips
-        walls = source_blocks([diagonal * 2 + c for c in range(2)], walls)
+        walls = source_blocks([diagonal + 1 - core], walls)
     else:
         walls = source_blocks(range(nb), walls)
     sign = jnp.where(lax.broadcasted_iota(jnp.int32, (scenarios, 128), 1) < NBLD, -1.0, 1.0)

time: 26.8 us -> 26.3 us (0.981)
  Pallas kernels: 26.6 us -> 26 us
    pallas_call x1, Pallas kernels: 23.4 us -> 22.9 us  [superpose(): pl.pallas_call(functools.partial(superpose_kernel, nb, nz, tloc * nz), ou...]
where the time goes in v5:
time: 26.3 us; the launch traced here: 26 us
  Pallas kernels  26 us (99%)
    pallas_call x1, Pallas kernels, superpose(): pl.pallas_call(functools.partial(superpose_kernel, nb, nz, tloc * nz), ou...  22.9 us
    pallas_call x1, Pallas kernels, inverse(): pl.pallas_call(functools.partial(inverse_kernel, hours), out_shape=jax.Sh...  3.18 us

profile of v5, /device:TPU:0, one launch (start us, length us, event | category | flops | bytes accessed | tf_op | source)
XLA Modules:
  0.0 26.0 jit_solution(14871358665507029896)
XLA Ops:
  0.0 22.9 %superpose.1.wall_v = f32[32,128]{1,0:T(8,128)S(1)} custom-call(s32[8]{0:T(128)} %freq_ref.3, s32[1,4096]{1,0:T(1,128)} %bitcast.1, bf16[16,64,2048]{2,1,0:T(8,128)(2,1)} %loads_hbm.1, bf16[2,2,512,4096]{3,2,1,0:T(8,128)(2,1)} %pair_hbm.1, bf16[128,512]{1,0:T(8,128)(2,1)} %share_hbm.1), custom_call_target="tpu_custom_call" | custom-call | tf_op jit(solution)/shard_map/superpose/pallas_call | solution.py:302
  22.9 3.2 %inverse.1 = bf16[4,64,8192]{2,1,0:T(8,128)(2,1)} custom-call(s32[8]{0:T(128)} %freq_ref.3, f32[32,128]{1,0:T(8,128)S(1)} %superpose.1.wall_v), custom_call_target="tpu_custom_call" | custom-call | tf_op jit(solution)/shard_map/inverse/pallas_call | solution.py:386

commit v6 on v4

--- a/solution.py
+++ b/solution.py
@@ -101,24 +101,27 @@
     cos, sin = cos_sin(harmonic_column(freq_ref, freqs), z * tloc, tloc, hours)
     table = jnp.concatenate([*halves(cos), *halves(sin)], 0)
     lanes = sp * NBLD
-    keep = lax.broadcasted_iota(jnp.int32, (sp, lanes), 1) // NBLD == lax.broadcasted_iota(jnp.int32, (sp, lanes), 0)
-    fold_from = lax.broadcasted_iota(jnp.int32, (lanes, 128), 0) % NBLD
-    fold_to = lax.broadcasted_iota(jnp.int32, (lanes, 128), 1)
-    folds = [(fold_from + c * NBLD == fold_to).astype(jnp.float32).astype(jnp.bfloat16) for c in range(2)]
-
     square = chips == 4
     over_x = chip + 1 - 2 * (chip % 2)
     over_y = (chip + 2) % chips
     first_hops = (over_x, over_y) if square else tuple((chip + r) % chips for r in range(1, chips))
     first_from = first_hops if square else tuple((chip + chips - r) % chips for r in range(1, chips))
+    every = slice(0, scenarios)
+    halves_of = [pl.ds(r * (scenarios // 2), scenarios // 2) for r in range(2)]
+    if square:
+        sends = [(halves_of[r], over) for r, over in enumerate(first_hops)]
+        sends += [(halves_of[1 - r], over) for r, over in enumerate(first_hops)]
+    else:
+        sends = [(every, over) for over in first_hops]
     share_copies = [
         pltpu.make_async_remote_copy(
-            src_ref=share_v.at[b], dst_ref=share_v.at[b], send_sem=sh_send.at[r], recv_sem=sh_recv.at[r],
+            src_ref=share_v.at[b, rows], dst_ref=share_v.at[b, rows], send_sem=sh_send.at[r], recv_sem=sh_recv.at[r],
             device_id=device, device_id_type=MESH,
         )
-        for r, device in enumerate([(to * 2 + core, z) for to in first_hops] + [(sibling, z)])
+        for r, (rows, device) in enumerate(
+            [(rows, (over * 2 + core, z)) for rows, over in sends] + [(every, (sibling, z))]
+        )
     ]
-
     for q in range(nb):
         piece = pl.ds(q * bloc, bloc)
         label = lax.broadcasted_iota(jnp.int32, (2 * NBLD, bloc), 0) % NBLD
@@ -139,15 +142,13 @@
             spec = spec + lax.dot_general(
                 table[:, h * hp : (h + 1) * hp], chunk, NT, preferred_element_type=jnp.float32
             )
-        total = jnp.zeros((freqs * sp, 128), jnp.float32)
-        for c in range(2):
-            upper, lower = spec[2 * c * freqs : (2 * c + 1) * freqs], spec[(2 * c + 1) * freqs : (2 * c + 2) * freqs]
-            part = (upper + lower) * ((1.0 - 2.0 * c) / math.sqrt(hours))
-            spread = jnp.concatenate(
-                [jnp.where(keep, part[k : k + 1], 0.0).astype(jnp.bfloat16) for k in range(freqs)], 0
-            )
-            total = total + jnp.dot(spread, folds[c], preferred_element_type=jnp.float32)
-        folded.append(total.reshape(freqs, sp, 128))
+        real = (spec[:freqs] + spec[freqs : 2 * freqs]) * (1.0 / math.sqrt(hours))
+        imag = (spec[2 * freqs : 3 * freqs] + spec[3 * freqs :]) * (-1.0 / math.sqrt(hours))
+        rows = [
+            jnp.concatenate([part[:, r * NBLD : (r + 1) * NBLD] for part in (real, imag)], 1)[None]
+            for r in range(sp)
+        ]
+        folded.append(jnp.swapaxes(jnp.concatenate(rows, 0), 0, 1))
     bs_stage[...] = jnp.concatenate(folded, 1).astype(jnp.bfloat16)
 
     bs_copies = []
@@ -163,6 +164,44 @@
         bs_copies[-1].start()
     bs_all[z, b] = bs_stage[z * FLOC + core]
 
+    here = sel_v[0:NBLD, pl.ds(pl.multiple_of(b * bloc, 128), bloc)]
+    width = 2048
+
+    cross_copies = []
+
+    def gather_away(d):
+        pair_copies[d].wait()
+
+        def step(i, carry):
+            piece = pl.ds(pl.multiple_of(i * width, width), width)
+            total = jnp.dot(here, pair_v[turns[0], d, :, piece], preferred_element_type=jnp.float32)
+            cross_stage[d, :, piece] = total.astype(jnp.bfloat16)
+            return carry
+
+        lax.fori_loop(0, bores // width, step, 0)
+        cross_copies.append(
+            pltpu.make_async_remote_copy(
+                src_ref=cross_stage.at[d], dst_ref=cross_recv.at[d], send_sem=cr_ssem.at[d], recv_sem=cr_rsem.at[d],
+                device_id=(sibling, z), device_id_type=MESH,
+            )
+        )
+        cross_copies[-1].start()
+
+    def gather_here(d):
+        pair_copies[2 + d].wait()
+        cross_copies[d].wait_recv()
+
+        def step(i, carry):
+            piece = pl.ds(pl.multiple_of(i * width, width), width)
+            total = jnp.dot(here, pair_v[turns[1], d, :, piece], preferred_element_type=jnp.float32)
+            total = total + cross_recv[d, :, piece].astype(jnp.float32)
+            grid_v[pl.ds(d * NBLD, NBLD), piece] = total.astype(jnp.bfloat16)
+            return carry
+
+        lax.fori_loop(0, bores // width, step, 0)
+
+    gather_away(0)
+
     fw_copies = []
 
     def forward(r, origin, rows, device):
@@ -175,64 +214,28 @@
         )
         fw_copies[-1].start()
 
-    here = sel_v[0:NBLD, pl.ds(pl.multiple_of(b * bloc, 128), bloc)]
-    width = 2048
-
-    cross_copies = []
-
-    def gather_away(d):
-        pair_copies[d].wait()
-
-        def step(i, carry):
-            piece = pl.ds(pl.multiple_of(i * width, width), width)
-            total = jnp.dot(here, pair_v[turns[0], d, :, piece], preferred_element_type=jnp.float32)
-            cross_stage[d, :, piece] = total.astype(jnp.bfloat16)
-            return carry
-
-        lax.fori_loop(0, bores // width, step, 0)
-        cross_copies.append(
-            pltpu.make_async_remote_copy(
-                src_ref=cross_stage.at[d], dst_ref=cross_recv.at[d], send_sem=cr_ssem.at[d], recv_sem=cr_rsem.at[d],
-                device_id=(sibling, z), device_id_type=MESH,
-            )
-        )
-        cross_copies[-1].start()
-
-    def gather_here(d):
-        pair_copies[2 + d].wait()
-        cross_copies[d].wait_recv()
-
-        def step(i, carry):
-            piece = pl.ds(pl.multiple_of(i * width, width), width)
-            total = jnp.dot(here, pair_v[turns[1], d, :, piece], preferred_element_type=jnp.float32)
-            total = total + cross_recv[d, :, piece].astype(jnp.float32)
-            grid_v[pl.ds(d * NBLD, NBLD), piece] = total.astype(jnp.bfloat16)
-            return carry
-
-        lax.fori_loop(0, bores // width, step, 0)
-
-    gather_away(0)
+    if square:
+        for r, origin in enumerate(first_from):
+            share_copies[r].wait_recv()
+            forward(chips + r, origin * 2 + core, halves_of[r], first_hops[1 - r] * 2 + core)
+
     gather_away(1)
 
-    every = slice(0, scenarios)
+    gather_here(0)
+
     for r, origin in enumerate(first_from):
-        share_copies[r].wait_recv()
-        if square:
-            rows = pl.ds(r * (scenarios // 2), scenarios // 2)
-            forward(chips + r, origin * 2 + core, rows, first_hops[1 - r] * 2 + core)
+        share_copies[2 + r if square else r].wait_recv()
         forward(r, origin * 2 + core, every, sibling)
 
-
-    gather_here(0)
     gather_here(1)
 
     if square:
+        diagonal = (over_x + 2) % chips * 2
         for r in range(2):
-            fw_copies[2 * r].wait_recv()
-        forward(2, (over_x + 2) % chips * 2 + core, every, sibling)
-
+            fw_copies[r].wait_recv()
+        forward(2, diagonal + core, every, sibling)
     share_copies[-1].wait_recv()
-    for copy in (fw_copies[1], fw_copies[3]) if square else fw_copies:
+    for copy in fw_copies[2:4] if square else fw_copies:
         copy.wait_recv()
     for copy in bs_copies:
         copy.wait_recv()
@@ -255,10 +258,9 @@
 
     walls = jnp.zeros((2 * scenarios, 128), jnp.float32)
     if square:
-        walls = source_blocks([q * 2 + c for q in (chip, over_x, over_y) for c in range(2)], walls)
+        walls = source_blocks([b, sibling, over_x * 2, over_x * 2 + 1, over_y * 2, over_y * 2 + 1, diagonal + core], walls)
         fw_copies[4].wait_recv()
-        diagonal = (over_x + 2) % chips
-        walls = source_blocks([diagonal * 2 + c for c in range(2)], walls)
+        walls = source_blocks([diagonal + 1 - core], walls)
     else:
         walls = source_blocks(range(nb), walls)
     sign = jnp.where(lax.broadcasted_iota(jnp.int32, (scenarios, 128), 1) < NBLD, -1.0, 1.0)
@@ -326,8 +328,8 @@
             dma((2, 2)),
             dma((FLOC, 2)),
             dma,
-            dma((nb // 2,)),
-            dma((nb // 2,)),
+            dma((nb // 2 + 1,)),
+            dma((nb // 2 + 1,)),
             dma((nb // 2 + 2,)),
             dma((nb // 2 + 2,)),
             dma((2,)),

time: 26.8 us -> 25.9 us (0.966)
  Pallas kernels: 26.6 us -> 25.6 us
    pallas_call x1, Pallas kernels: 23.4 us -> 22.4 us  [superpose(): pl.pallas_call(functools.partial(superpose_kernel, nb, nz, tloc * nz), ou...]
where the time goes in v6:
time: 25.9 us; the launch traced here: 25.6 us
  Pallas kernels  25.6 us (99%)
    pallas_call x1, Pallas kernels, superpose(): pl.pallas_call(functools.partial(superpose_kernel, nb, nz, tloc * nz), ou...  22.4 us
    pallas_call x1, Pallas kernels, inverse(): pl.pallas_call(functools.partial(inverse_kernel, hours), out_shape=jax.Sh...  3.18 us

profile of v6, /device:TPU:0, one launch (start us, length us, event | category | flops | bytes accessed | tf_op | source)
XLA Modules:
  0.0 25.6 jit_solution(18195775664458043105)
XLA Ops:
  0.0 22.4 %superpose.1.wall_v = f32[32,128]{1,0:T(8,128)S(1)} custom-call(s32[8]{0:T(128)} %freq_ref.3, s32[1,4096]{1,0:T(1,128)} %bitcast.1, bf16[16,64,2048]{2,1,0:T(8,128)(2,1)} %loads_hbm.1, bf16[2,2,512,4096]{3,2,1,0:T(8,128)(2,1)} %pair_hbm.1, bf16[128,512]{1,0:T(8,128)(2,1)} %share_hbm.1), custom_call_target="tpu_custom_call" | custom-call | tf_op jit(solution)/shard_map/superpose/pallas_call | solution.py:305
  22.4 3.2 %inverse.1 = bf16[4,64,8192]{2,1,0:T(8,128)(2,1)} custom-call(s32[8]{0:T(128)} %freq_ref.3, f32[32,128]{1,0:T(8,128)S(1)} %superpose.1.wall_v), custom_call_target="tpu_custom_call" | custom-call | tf_op jit(solution)/shard_map/inverse/pallas_call | solution.py:389

commit v7 on v6

--- a/solution.py
+++ b/solution.py
@@ -245,49 +245,50 @@
         spec_all = spec_all + bs_all[k].astype(jnp.float32)
     spec_all = spec_all.reshape(scenarios, 128)
     half = lax.broadcasted_iota(jnp.int32, (scenarios, 128), 1) // NBLD
-    spec_c = jnp.concatenate([jnp.where(half == c, spec_all, 0.0).astype(jnp.bfloat16) for c in range(2)], 0)
-
-    def source_blocks(origins, walls):
+    sign = jnp.where(lax.broadcasted_iota(jnp.int32, (scenarios // 2, 128), 1) < NBLD, -1.0, 1.0)
+    slot = z * FLOC + core
+    me = b * nz + z
+    others = [j + (me <= j).astype(jnp.int32) for j in range(nb * nz - 1)]
+
+    def wall_copy(to, source):
+        return pltpu.make_async_remote_copy(
+            src_ref=wall_stage.at[to], dst_ref=wall_recv.at[slot, chip],
+            send_sem=wl_ssem.at[to], recv_sem=wl_rsem.at[source],
+            device_id=(to // nz, to % nz), device_id_type=MESH,
+        )
+
+    def source_blocks(part, origins, walls):
+        rows = slice(part * (scenarios // 2), (part + 1) * (scenarios // 2))
+        spec_c = jnp.concatenate(
+            [jnp.where(half[rows] == c, spec_all[rows], 0.0).astype(jnp.bfloat16) for c in range(2)], 0
+        )
         for q in origins:
             piece = pl.ds(pl.multiple_of(q * bloc, 128), bloc)
-            weight = share_v[q].astype(jnp.float32)
+            weight = share_v[q, rows].astype(jnp.float32)
             picked = jnp.dot(spec_c, sel_v[:, piece], preferred_element_type=jnp.float32)
-            source = (picked.reshape(2, scenarios, bloc) * weight).astype(jnp.bfloat16).reshape(2 * scenarios, bloc)
+            source = (picked.reshape(2, scenarios // 2, bloc) * weight).astype(jnp.bfloat16).reshape(scenarios, bloc)
             walls = walls + lax.dot_general(source, grid_v[:, piece], NT, preferred_element_type=jnp.float32)
         return walls
 
-    walls = jnp.zeros((2 * scenarios, 128), jnp.float32)
-    if square:
-        walls = source_blocks([b, sibling, over_x * 2, over_x * 2 + 1, over_y * 2, over_y * 2 + 1, diagonal + core], walls)
-        fw_copies[4].wait_recv()
-        walls = source_blocks([diagonal + 1 - core], walls)
-    else:
-        walls = source_blocks(range(nb), walls)
-    sign = jnp.where(lax.broadcasted_iota(jnp.int32, (scenarios, 128), 1) < NBLD, -1.0, 1.0)
-    joined = (walls[:scenarios] + sign * pltpu.roll(walls[scenarios:], NBLD, 1)) * (NBLD / bores)
-    wall_stage[...] = joined.reshape(nb * nz, s4, 128)
-
-    slot = z * FLOC + core
-    def wall_copy(r, to_z, from_z):
-        to_b = (b + r) % nb
-        return pltpu.make_async_remote_copy(
-            src_ref=wall_stage.at[to_b * nz + to_z], dst_ref=wall_recv.at[slot, chip],
-            send_sem=wl_ssem.at[r, to_z], recv_sem=wl_rsem.at[r, from_z],
-            device_id=(to_b, to_z), device_id_type=MESH,
-        )
-
-    plane_first = []
-    for k in range(nz):
-        plane_first += [(r, k) for r in range(1, nb)]
-        if k < nz - 1:
-            plane_first.append((0, k + (z <= k).astype(jnp.int32)))
-    for r, k in plane_first:
-        wall_copy(r, k, z).start()
+    mid = nb * nz // 2
+    for part in range(2):
+        walls = jnp.zeros((scenarios, 128), jnp.float32)
+        if square and part == 0:
+            near = [q * 2 + c for q in (chip, over_x, over_y) for c in range(2)]
+            walls = source_blocks(part, [*near, diagonal + core], walls)
+            fw_copies[4].wait_recv()
+            walls = source_blocks(part, [diagonal + 1 - core], walls)
+        else:
+            walls = source_blocks(part, range(nb), walls)
+        joined = walls[: scenarios // 2] + sign * pltpu.roll(walls[scenarios // 2 :], NBLD, 1)
+        wall_stage[pl.ds(part * mid, mid)] = (joined * (NBLD / bores)).reshape(mid, s4, 128)
+        for to in others[mid - 1 :] if part else others[: mid - 1]:
+            wall_copy(to, me).start()
     wall_recv[slot, chip] = wall_stage[b * nz + z]
     for copy in share_copies + bs_copies + fw_copies + cross_copies:
         copy.wait_send()
-    for r, k in plane_first:
-        wall_copy(r, k, k).wait()
+    for other in others:
+        wall_copy(other, other).wait()
     wall = wall_recv[:, 0]
     for q in range(1, chips):
         wall = wall + wall_recv[:, q]
@@ -336,8 +337,8 @@
             dma((2,)),
             dma((nb, nz)),
             dma((nb, nz)),
-            dma((nb, nz)),
-            dma((nb, nz)),
+            dma((nb * nz,)),
+            dma((nb * nz,)),
         ],
         compiler_params=pltpu.CompilerParams(
             collective_id=0, has_side_effects=True, vmem_limit_bytes=56 * 2**20

time: 25.9 us -> 25.3 us (0.977)
  Pallas kernels: 25.6 us -> 25.1 us
    pallas_call x1, Pallas kernels: 22.4 us -> 21.9 us  [superpose(): pl.pallas_call(functools.partial(superpose_kernel, nb, nz, tloc * nz), ou...]
where the time goes in v7:
time: 25.3 us; the launch traced here: 25.1 us
  Pallas kernels  25.1 us (99%)
    pallas_call x1, Pallas kernels, superpose(): pl.pallas_call(functools.partial(superpose_kernel, nb, nz, tloc * nz), ou...  21.9 us
    pallas_call x1, Pallas kernels, inverse(): pl.pallas_call(functools.partial(inverse_kernel, hours), out_shape=jax.Sh...  3.18 us

profile of v7, /device:TPU:0, one launch (start us, length us, event | category | flops | bytes accessed | tf_op | source)
XLA Modules:
  0.0 25.1 jit_solution(17210882641321411998)
XLA Ops:
  0.0 21.9 %superpose.1.wall_v = f32[32,128]{1,0:T(8,128)S(1)} custom-call(s32[8]{0:T(128)} %freq_ref.3, s32[1,4096]{1,0:T(1,128)} %bitcast.1, bf16[16,64,2048]{2,1,0:T(8,128)(2,1)} %loads_hbm.1, bf16[2,2,512,4096]{3,2,1,0:T(8,128)(2,1)} %pair_hbm.1, bf16[128,512]{1,0:T(8,128)(2,1)} %share_hbm.1), custom_call_target="tpu_custom_call" | custom-call | tf_op jit(solution)/shard_map/superpose/pallas_call | solution.py:306
  21.9 3.2 %inverse.1 = bf16[4,64,8192]{2,1,0:T(8,128)(2,1)} custom-call(s32[8]{0:T(128)} %freq_ref.3, f32[32,128]{1,0:T(8,128)S(1)} %superpose.1.wall_v), custom_call_target="tpu_custom_call" | custom-call | tf_op jit(solution)/shard_map/inverse/pallas_call | solution.py:390

commit v8 on v7

--- a/solution.py
+++ b/solution.py
@@ -151,17 +151,18 @@
         folded.append(jnp.swapaxes(jnp.concatenate(rows, 0), 0, 1))
     bs_stage[...] = jnp.concatenate(folded, 1).astype(jnp.bfloat16)
 
-    bs_copies = []
-    for r, k in near_first[::-1]:
-        to_b, to_z = (b + r) % nb, (z + k) % nz
-        bs_copies.append(
-            pltpu.make_async_remote_copy(
-                src_ref=bs_stage.at[to_z * FLOC + to_b % 2], dst_ref=bs_all.at[z, b],
-                send_sem=bs_ssem.at[r, k], recv_sem=bs_rsem.at[r, k],
-                device_id=(to_b, to_z), device_id_type=MESH,
-            )
-        )
-        bs_copies[-1].start()
+    me = b * nz + z
+    others = [j + (me <= j).astype(jnp.int32) for j in range(nb * nz - 1)]
+
+    def spec_copy(to, source):
+        return pltpu.make_async_remote_copy(
+            src_ref=bs_stage.at[to % nz * FLOC + to // nz % 2], dst_ref=bs_all.at[z, b],
+            send_sem=bs_ssem.at[to], recv_sem=bs_rsem.at[source],
+            device_id=(to // nz, to % nz), device_id_type=MESH,
+        )
+
+    for to in others[::-1]:
+        spec_copy(to, me).start()
     bs_all[z, b] = bs_stage[z * FLOC + core]
 
     here = sel_v[0:NBLD, pl.ds(pl.multiple_of(b * bloc, 128), bloc)]
@@ -237,18 +238,9 @@
     share_copies[-1].wait_recv()
     for copy in fw_copies[2:4] if square else fw_copies:
         copy.wait_recv()
-    for copy in bs_copies:
-        copy.wait_recv()
-
-    spec_all = bs_all[0].astype(jnp.float32)
-    for k in range(1, nz):
-        spec_all = spec_all + bs_all[k].astype(jnp.float32)
-    spec_all = spec_all.reshape(scenarios, 128)
-    half = lax.broadcasted_iota(jnp.int32, (scenarios, 128), 1) // NBLD
+    half = lax.broadcasted_iota(jnp.int32, (scenarios // 2, 128), 1) // NBLD
     sign = jnp.where(lax.broadcasted_iota(jnp.int32, (scenarios // 2, 128), 1) < NBLD, -1.0, 1.0)
     slot = z * FLOC + core
-    me = b * nz + z
-    others = [j + (me <= j).astype(jnp.int32) for j in range(nb * nz - 1)]
 
     def wall_copy(to, source):
         return pltpu.make_async_remote_copy(
@@ -257,11 +249,8 @@
             device_id=(to // nz, to % nz), device_id_type=MESH,
         )
 
-    def source_blocks(part, origins, walls):
+    def source_blocks(part, spec_c, origins, walls):
         rows = slice(part * (scenarios // 2), (part + 1) * (scenarios // 2))
-        spec_c = jnp.concatenate(
-            [jnp.where(half[rows] == c, spec_all[rows], 0.0).astype(jnp.bfloat16) for c in range(2)], 0
-        )
         for q in origins:
             piece = pl.ds(pl.multiple_of(q * bloc, 128), bloc)
             weight = share_v[q, rows].astype(jnp.float32)
@@ -272,20 +261,30 @@
 
     mid = nb * nz // 2
     for part in range(2):
+        for other in others[mid:] if part else others[:mid]:
+            spec_copy(other, other).wait_recv()
+        blocks = slice(part * (nb // 2), (part + 1) * (nb // 2))
+        spec = bs_all[0, blocks].astype(jnp.float32)
+        for k in range(1, nz):
+            spec = spec + bs_all[k, blocks].astype(jnp.float32)
+        spec = spec.reshape(scenarios // 2, 128)
+        spec_c = jnp.concatenate([jnp.where(half == c, spec, 0.0).astype(jnp.bfloat16) for c in range(2)], 0)
         walls = jnp.zeros((scenarios, 128), jnp.float32)
         if square and part == 0:
             near = [q * 2 + c for q in (chip, over_x, over_y) for c in range(2)]
-            walls = source_blocks(part, [*near, diagonal + core], walls)
+            walls = source_blocks(part, spec_c, [*near, diagonal + core], walls)
             fw_copies[4].wait_recv()
-            walls = source_blocks(part, [diagonal + 1 - core], walls)
+            walls = source_blocks(part, spec_c, [diagonal + 1 - core], walls)
         else:
-            walls = source_blocks(part, range(nb), walls)
+            walls = source_blocks(part, spec_c, range(nb), walls)
         joined = walls[: scenarios // 2] + sign * pltpu.roll(walls[scenarios // 2 :], NBLD, 1)
         wall_stage[pl.ds(part * mid, mid)] = (joined * (NBLD / bores)).reshape(mid, s4, 128)
         for to in others[mid - 1 :] if part else others[: mid - 1]:
             wall_copy(to, me).start()
     wall_recv[slot, chip] = wall_stage[b * nz + z]
-    for copy in share_copies + bs_copies + fw_copies + cross_copies:
+    for other in others:
+        spec_copy(other, other).wait_send()
+    for copy in share_copies + fw_copies + cross_copies:
         copy.wait_send()
     for other in others:
         wall_copy(other, other).wait()
@@ -335,8 +334,8 @@
             dma((nb // 2 + 2,)),
             dma((2,)),
             dma((2,)),
-            dma((nb, nz)),
-            dma((nb, nz)),
+            dma((nb * nz,)),
+            dma((nb * nz,)),
             dma((nb * nz,)),
             dma((nb * nz,)),
         ],

time: 25.3 us -> 25.1 us (level)
  Pallas kernels: 25.1 us -> 24.8 us
where the time goes in v8:
time: 25.1 us; the launch traced here: 24.8 us
  Pallas kernels  24.8 us (99%)
    pallas_call x1, Pallas kernels, superpose(): pl.pallas_call(functools.partial(superpose_kernel, nb, nz, tloc * nz), ou...  21.6 us
    pallas_call x1, Pallas kernels, inverse(): pl.pallas_call(functools.partial(inverse_kernel, hours), out_shape=jax.Sh...  3.18 us

profile of v8, /device:TPU:0, one launch (start us, length us, event | category | flops | bytes accessed | tf_op | source)
XLA Modules:
  0.0 24.8 jit_solution(2797453895334114564)
XLA Ops:
  0.0 21.6 %superpose.1.wall_v = f32[32,128]{1,0:T(8,128)S(1)} custom-call(s32[8]{0:T(128)} %freq_ref.3, s32[1,4096]{1,0:T(1,128)} %bitcast.1, bf16[16,64,2048]{2,1,0:T(8,128)(2,1)} %loads_hbm.1, bf16[2,2,512,4096]{3,2,1,0:T(8,128)(2,1)} %pair_hbm.1, bf16[128,512]{1,0:T(8,128)(2,1)} %share_hbm.1), custom_call_target="tpu_custom_call" | custom-call | tf_op jit(solution)/shard_map/superpose/pallas_call | solution.py:305
  21.6 3.2 %inverse.1 = bf16[4,64,8192]{2,1,0:T(8,128)(2,1)} custom-call(s32[8]{0:T(128)} %freq_ref.3, f32[32,128]{1,0:T(8,128)S(1)} %superpose.1.wall_v), custom_call_target="tpu_custom_call" | custom-call | tf_op jit(solution)/shard_map/inverse/pallas_call | solution.py:389

commit v9 on v8

--- a/solution.py
+++ b/solution.py
@@ -166,7 +166,7 @@
     bs_all[z, b] = bs_stage[z * FLOC + core]
 
     here = sel_v[0:NBLD, pl.ds(pl.multiple_of(b * bloc, 128), bloc)]
-    width = 2048
+    width = 4096
 
     cross_copies = []
 
@@ -232,9 +232,8 @@
 
     if square:
         diagonal = (over_x + 2) % chips * 2
-        for r in range(2):
-            fw_copies[r].wait_recv()
-        forward(2, diagonal + core, every, sibling)
+        fw_copies[0].wait_recv()
+        forward(2, diagonal + core, halves_of[0], sibling)
     share_copies[-1].wait_recv()
     for copy in fw_copies[2:4] if square else fw_copies:
         copy.wait_recv()
@@ -273,9 +272,13 @@
         if square and part == 0:
             near = [q * 2 + c for q in (chip, over_x, over_y) for c in range(2)]
             walls = source_blocks(part, spec_c, [*near, diagonal + core], walls)
+            fw_copies[1].wait_recv()
+            forward(3, diagonal + core, halves_of[1], sibling)
             fw_copies[4].wait_recv()
             walls = source_blocks(part, spec_c, [diagonal + 1 - core], walls)
         else:
+            if square:
+                fw_copies[5].wait_recv()
             walls = source_blocks(part, spec_c, range(nb), walls)
         joined = walls[: scenarios // 2] + sign * pltpu.roll(walls[scenarios // 2 :], NBLD, 1)
         wall_stage[pl.ds(part * mid, mid)] = (joined * (NBLD / bores)).reshape(mid, s4, 128)

time: 25.1 us -> 24.9 us (level)
  no operation moved by 1% of the time
where the time goes in v9:
time: 24.9 us; the launch traced here: 24.7 us
  Pallas kernels  24.7 us (99%)
    pallas_call x1, Pallas kernels, superpose(): pl.pallas_call(functools.partial(superpose_kernel, nb, nz, tloc * nz), ou...  21.5 us
    pallas_call x1, Pallas kernels, inverse(): pl.pallas_call(functools.partial(inverse_kernel, hours), out_shape=jax.Sh...  3.18 us

profile of v9, /device:TPU:0, one launch (start us, length us, event | category | flops | bytes accessed | tf_op | source)
XLA Modules:
  0.0 24.7 jit_solution(732735668636255830)
XLA Ops:
  0.0 21.5 %superpose.1.wall_v = f32[32,128]{1,0:T(8,128)S(1)} custom-call(s32[8]{0:T(128)} %freq_ref.3, s32[1,4096]{1,0:T(1,128)} %bitcast.1, bf16[16,64,2048]{2,1,0:T(8,128)(2,1)} %loads_hbm.1, bf16[2,2,512,4096]{3,2,1,0:T(8,128)(2,1)} %pair_hbm.1, bf16[128,512]{1,0:T(8,128)(2,1)} %share_hbm.1), custom_call_target="tpu_custom_call" | custom-call | tf_op jit(solution)/shard_map/superpose/pallas_call | solution.py:308
  21.5 3.2 %inverse.1 = bf16[4,64,8192]{2,1,0:T(8,128)(2,1)} custom-call(s32[8]{0:T(128)} %freq_ref.3, f32[32,128]{1,0:T(8,128)S(1)} %superpose.1.wall_v), custom_call_target="tpu_custom_call" | custom-call | tf_op jit(solution)/shard_map/inverse/pallas_call | solution.py:392
